TPU v7x, 32 devices: a whole 2x2x4 slice. The times are simulated.
32 devices in a mesh: dp: 4 (over x, core), seq: 2 (over y), tensor: 4 (over z).
Axes of the slice: x: 2, y: 2, z: 4, core: 2. Of those that a mesh axis runs over, the one named last changes fastest.
Arguments:
- frames: bfloat16 [4, 1024, 768], P('dp', 'seq'), may hold values from -6 to 6
- cotangent: bfloat16 [4, 1024, 768], P('dp', 'seq'), may hold values from -6 to 6
- heads_weight: float32 [2, 768, 3, 768], P(None, ('dp', 'seq'), None, 'tensor'), may hold values from -0.3125 to 0.3125
- merge_weight: float32 [2, 768, 768], P(None, ('dp', 'seq'), 'tensor'), may hold values from -0.21875 to 0.21875
- expand_weight: float32 [2, 768, 4, 768], P(None, ('dp', 'seq'), None, 'tensor'), may hold values from -0.21875 to 0.21875
- shrink_weight: float32 [2, 768, 4, 768], P(None, ('dp', 'seq'), None, 'tensor'), may hold values from -0.21875 to 0.21875
- shared_vectors: float32 [2, 6, 768], replicated, may hold values from -1.2 to 1.2, as said below
- split_vectors: float32 [2, 6, 768], P(None, None, 'tensor'), may hold values from -1.2 to 1.2
- heads_first: float32 [2, 768, 3, 768], P(None, ('dp', 'seq'), None, 'tensor')
- heads_second: float32 [2, 768, 3, 768], P(None, ('dp', 'seq'), None, 'tensor'), as said below
- merge_first: float32 [2, 768, 768], P(None, ('dp', 'seq'), 'tensor')
- merge_second: float32 [2, 768, 768], P(None, ('dp', 'seq'), 'tensor'), as said below
- expand_first: float32 [2, 768, 4, 768], P(None, ('dp', 'seq'), None, 'tensor')
- expand_second: float32 [2, 768, 4, 768], P(None, ('dp', 'seq'), None, 'tensor'), as said below
- shrink_first: float32 [2, 768, 4, 768], P(None, ('dp', 'seq'), None, 'tensor')
- shrink_second: float32 [2, 768, 4, 768], P(None, ('dp', 'seq'), None, 'tensor'), as said below
- shared_first: float32 [2, 6, 768], replicated
- shared_second: float32 [2, 6, 768], replicated, as said below
- split_first: float32 [2, 6, 768], P(None, None, 'tensor')
- split_second: float32 [2, 6, 768], P(None, None, 'tensor'), as said below
Outputs:
- encoded: float32 [4, 1024, 768], P('dp', 'seq')
- input_grad: float32 [4, 1024, 768], P('dp', 'seq')
- heads_grad: float32 [2, 768, 3, 768], P(None, ('dp', 'seq'), None, 'tensor')
- heads_renewed: float32 [2, 768, 3, 768], P(None, ('dp', 'seq'), None, 'tensor')
- heads_updated: float32 [2, 768, 3, 768], P(None, ('dp', 'seq'), None, 'tensor')
- merge_grad: float32 [2, 768, 768], P(None, ('dp', 'seq'), 'tensor')
- merge_renewed: float32 [2, 768, 768], P(None, ('dp', 'seq'), 'tensor')
- merge_updated: float32 [2, 768, 768], P(None, ('dp', 'seq'), 'tensor')
- expand_grad: float32 [2, 768, 4, 768], P(None, ('dp', 'seq'), None, 'tensor')
- expand_renewed: float32 [2, 768, 4, 768], P(None, ('dp', 'seq'), None, 'tensor')
- expand_updated: float32 [2, 768, 4, 768], P(None, ('dp', 'seq'), None, 'tensor')
- shrink_grad: float32 [2, 768, 4, 768], P(None, ('dp', 'seq'), None, 'tensor')
- shrink_renewed: float32 [2, 768, 4, 768], P(None, ('dp', 'seq'), None, 'tensor')
- shrink_updated: float32 [2, 768, 4, 768], P(None, ('dp', 'seq'), None, 'tensor')
- shared_grad: float32 [2, 6, 768], replicated
- shared_renewed: float32 [2, 6, 768], replicated
- shared_updated: float32 [2, 6, 768], replicated
- split_grad: float32 [2, 6, 768], P(None, None, 'tensor')
- split_renewed: float32 [2, 6, 768], P(None, None, 'tensor')
- split_updated: float32 [2, 6, 768], P(None, None, 'tensor')
Inputs may be any that keep to these rules, and one draw needn't show every extreme that they name: `shared_vectors`: norm gains lie in 0.8 to 1.2, the other rows are biases. `heads_second`: positive. `merge_second`: positive. `expand_second`: positive. `shrink_second`: positive. `shared_second`: positive. `split_second`: positive.
All inputs are finite; a program needn't handle non-finite values.
Results may differ from a plain program's by a relative error of at most 0.023.
Values may be sent and summed in bfloat16 or wider, within the bound.
A program may use at most 128 MiB of HBM per device.

v0:
```python
import jax
import jax.numpy as jnp
from jax import lax
from jax.sharding import PartitionSpec as P

HEAD_DIM = 64
STEP = 10


beta_one = 0.9
beta_two = 0.999
adam_epsilon = 1e-08
weight_decay = 0.01
norm_epsilon = 1e-05


def layer_norm(values, gain_row, shift_row):
    centre = values - jnp.mean(values, axis=-1, keepdims=True)
    spread = jnp.mean(centre * centre, axis=-1, keepdims=True)
    return centre * lax.rsqrt(spread + norm_epsilon) * gain_row + shift_row


def gelu_exact(values):
    return jax.nn.gelu(values, approximate=False)


def attend_forward(inputs):
    query_rows, key_rows, value_rows = inputs
    scaling = HEAD_DIM ** (-0.5)
    scores = (
        jnp.einsum("qhc,khc->hqk", query_rows, key_rows, preferred_element_type=jnp.float32)
        * scaling
    )
    highest = jnp.max(scores, axis=-1, keepdims=True)
    weights = jnp.exp(scores - highest)
    totals = jnp.sum(weights, axis=-1, keepdims=True)
    shares = (weights / totals).astype(jnp.bfloat16)
    context = jnp.einsum("hqk,khc->qhc", shares, value_rows, preferred_element_type=jnp.float32)
    return (context, highest + jnp.log(totals))


def attend_backward(inputs):
    query_rows, key_rows, value_rows, log_totals, grad_context = inputs
    scaling = HEAD_DIM ** (-0.5)
    scores = (
        jnp.einsum("qhc,khc->hqk", query_rows, key_rows, preferred_element_type=jnp.float32)
        * scaling
    )
    shares = jnp.exp(scores - log_totals)
    grad_shares = jnp.einsum(
        "qhc,khc->hqk", grad_context, value_rows, preferred_element_type=jnp.float32
    )
    inner_sum = jnp.sum(shares * grad_shares, axis=-1, keepdims=True)
    grad_scores = (shares * (grad_shares - inner_sum)).astype(jnp.bfloat16)
    grad_query = (
        jnp.einsum("hqk,khc->qhc", grad_scores, key_rows, preferred_element_type=jnp.float32)
        * scaling
    )
    grad_key = (
        jnp.einsum("hqk,qhc->khc", grad_scores, query_rows, preferred_element_type=jnp.float32)
        * scaling
    )
    grad_value = jnp.einsum(
        "hqk,qhc->khc",
        shares.astype(jnp.bfloat16),
        grad_context,
        preferred_element_type=jnp.float32,
    )
    return (grad_query, grad_key, grad_value)


def head_total(partial_sum):
    return lax.psum(partial_sum, "tensor")


def back_total(partial_sum):
    return lax.psum(partial_sum, "tensor")


def adam_update(weight, gradient, first_moment, second, step_rate):
    first_new = beta_one * first_moment + (1.0 - beta_one) * gradient
    second_new = beta_two * second + (1.0 - beta_two) * gradient * gradient
    bias_one = 1.0 - beta_one**STEP
    bias_two = 1.0 - beta_two**STEP
    direction = first_new / bias_one / (jnp.sqrt(second_new / bias_two) + adam_epsilon)
    return (second_new, weight - step_rate * (direction + weight_decay * weight))


def stack_member(groups, member):
    return jnp.stack([group_item[member] for group_item in groups])


def shards(
    frames,
    cotangent,
    heads_weight,
    merge_weight,
    expand_weight,
    shrink_weight,
    shared_vectors,
    split_vectors,
    heads_first,
    heads_second,
    merge_first,
    merge_second,
    expand_first,
    expand_second,
    shrink_first,
    shrink_second,
    shared_first,
    shared_second,
    split_first,
    split_second,
):
    gathered = (
        lax.all_gather(heads_weight.astype(jnp.bfloat16), ("dp", "seq"), axis=1, tiled=True),
        lax.all_gather(merge_weight.astype(jnp.bfloat16), ("dp", "seq"), axis=1, tiled=True),
        lax.all_gather(expand_weight.astype(jnp.bfloat16), ("dp", "seq"), axis=1, tiled=True),
        lax.all_gather(shrink_weight.astype(jnp.bfloat16), ("dp", "seq"), axis=1, tiled=True),
    )
    clip_count, frame_count, model_width = frames.shape
    token_count = clip_count * frame_count
    local_width = split_vectors.shape[2]
    local_heads = local_width // HEAD_DIM
    hidden_local = 4 * local_width
    layer_count = heads_weight.shape[0]
    stream = frames.astype(jnp.float32).reshape(token_count, model_width)
    kept_layers = []
    for layer_index in range(layer_count):
        heads_full = gathered[0][layer_index]
        merge_full = gathered[1][layer_index]
        expand_full = gathered[2][layer_index].reshape(model_width, hidden_local)
        shrink_full = gathered[3][layer_index].reshape(model_width, hidden_local)
        shared = shared_vectors[layer_index]
        split_rows = split_vectors[layer_index]
        normed = layer_norm(stream, shared[0], shared[1]).astype(jnp.bfloat16)
        project = jnp.einsum("td,dke->tke", normed, heads_full, preferred_element_type=jnp.float32)
        query_rows = (project[:, 0] + split_rows[0]).astype(jnp.bfloat16)
        key_local = project[:, 1].astype(jnp.bfloat16).reshape(clip_count, frame_count, local_width)
        value_local = (
            (project[:, 2] + split_rows[1])
            .astype(jnp.bfloat16)
            .reshape(clip_count, frame_count, local_width)
        )
        key_rows, value_rows = (
            lax.all_gather(key_local, "seq", axis=1, tiled=True),
            lax.all_gather(value_local, "seq", axis=1, tiled=True),
        )
        full_frames = key_rows.shape[1]
        query_blocks = query_rows.reshape(clip_count, frame_count, local_heads, HEAD_DIM)
        context, log_totals = lax.map(
            attend_forward,
            (
                query_blocks,
                key_rows.reshape(clip_count, full_frames, local_heads, HEAD_DIM),
                value_rows.reshape(clip_count, full_frames, local_heads, HEAD_DIM),
            ),
        )
        context = context.reshape(token_count, local_width).astype(jnp.bfloat16)
        attended = head_total(
            jnp.einsum("te,oe->to", context, merge_full, preferred_element_type=jnp.float32)
        )
        middle = stream + attended + shared[2]
        normed_two = layer_norm(middle, shared[3], shared[4]).astype(jnp.bfloat16)
        preact = jnp.einsum(
            "td,df->tf", normed_two, expand_full, preferred_element_type=jnp.float32
        ) + split_rows[2:].reshape(hidden_local)
        hidden = gelu_exact(preact).astype(jnp.bfloat16)
        branch_out = head_total(
            jnp.einsum("tf,of->to", hidden, shrink_full, preferred_element_type=jnp.float32)
        )
        kept_keys, kept_values = (key_rows, value_rows)
        kept_layers.append(
            (
                stream,
                normed,
                query_blocks,
                kept_keys,
                kept_values,
                log_totals,
                context,
                middle,
                normed_two,
                preact,
            )
        )
        stream = middle + branch_out + shared[5]
    encoded = stream.reshape(clip_count, frame_count, model_width)
    grad_stream = cotangent.astype(jnp.float32).reshape(token_count, model_width)
    weight_groups = [None] * layer_count
    shared_groups = [None] * layer_count
    split_groups = [None] * layer_count
    for layer_index in reversed(range(layer_count)):
        (
            stream_in,
            normed,
            query_blocks,
            kept_keys,
            kept_values,
            log_totals,
            context,
            middle,
            normed_two,
            preact,
        ) = kept_layers[layer_index]
        heads_full = gathered[0][layer_index]
        merge_full = gathered[1][layer_index]
        expand_full = gathered[2][layer_index].reshape(model_width, hidden_local)
        shrink_full = gathered[3][layer_index].reshape(model_width, hidden_local)
        shared = shared_vectors[layer_index]
        key_rows, value_rows = (kept_keys, kept_values)
        full_frames = key_rows.shape[1]
        grad_low = grad_stream.astype(jnp.bfloat16)
        hidden = gelu_exact(preact).astype(jnp.bfloat16)
        grad_shrink = jnp.einsum("to,tf->of", grad_low, hidden, preferred_element_type=jnp.float32)
        grad_hidden = jnp.einsum(
            "to,of->tf", grad_low, shrink_full, preferred_element_type=jnp.float32
        )
        unused, gelu_pull = jax.vjp(gelu_exact, preact)
        grad_pre = gelu_pull(grad_hidden)[0].astype(jnp.bfloat16)
        grad_expand = jnp.einsum(
            "td,tf->df", normed_two, grad_pre, preferred_element_type=jnp.float32
        )
        grad_normed_two = back_total(
            jnp.einsum("tf,df->td", grad_pre, expand_full, preferred_element_type=jnp.float32)
        )
        unused, norm_pull_two = jax.vjp(layer_norm, middle, shared[3], shared[4])
        grad_middle_norm, grad_gain_two, grad_shift_two = norm_pull_two(grad_normed_two)
        grad_middle = grad_stream + grad_middle_norm
        grad_attn = grad_middle.astype(jnp.bfloat16)
        grad_merge = jnp.einsum("to,te->oe", grad_attn, context, preferred_element_type=jnp.float32)
        grad_context = jnp.einsum(
            "to,oe->te", grad_attn, merge_full, preferred_element_type=jnp.float32
        ).astype(jnp.bfloat16)
        grad_query, grad_key, grad_value = lax.map(
            attend_backward,
            (
                query_blocks,
                key_rows.reshape(clip_count, full_frames, local_heads, HEAD_DIM),
                value_rows.reshape(clip_count, full_frames, local_heads, HEAD_DIM),
                log_totals,
                grad_context.reshape(clip_count, frame_count, local_heads, HEAD_DIM),
            ),
        )
        grad_key_local, grad_value_local = (
            lax.psum_scatter(
                grad_key.reshape(clip_count, full_frames, local_width),
                "seq",
                scatter_dimension=1,
                tiled=True,
            ),
            lax.psum_scatter(
                grad_value.reshape(clip_count, full_frames, local_width),
                "seq",
                scatter_dimension=1,
                tiled=True,
            ),
        )
        grad_stack = jnp.stack(
            [
                grad_query.reshape(token_count, local_width),
                grad_key_local.reshape(token_count, local_width),
                grad_value_local.reshape(token_count, local_width),
            ],
            axis=1,
        ).astype(jnp.bfloat16)
        grad_heads = jnp.einsum(
            "td,tke->dke", normed, grad_stack, preferred_element_type=jnp.float32
        )
        grad_normed_one = back_total(
            jnp.einsum("tke,dke->td", grad_stack, heads_full, preferred_element_type=jnp.float32)
        )
        unused, norm_pull_one = jax.vjp(layer_norm, stream_in, shared[0], shared[1])
        grad_in_norm, grad_gain_one, grad_shift_one = norm_pull_one(grad_normed_one)
        shared_groups[layer_index] = jnp.stack(
            [
                grad_gain_one,
                grad_shift_one,
                jnp.sum(grad_middle, axis=0),
                grad_gain_two,
                grad_shift_two,
                jnp.sum(grad_stream, axis=0),
            ]
        )
        bias_pair = jnp.stack(
            [
                jnp.sum(grad_stack[:, 0], axis=0, dtype=jnp.float32),
                jnp.sum(grad_stack[:, 2], axis=0, dtype=jnp.float32),
            ]
        )
        split_groups[layer_index] = jnp.concatenate(
            [bias_pair, jnp.sum(grad_pre, axis=0, dtype=jnp.float32).reshape(4, local_width)],
            axis=0,
        )
        expand_grid = grad_expand.reshape(model_width, 4, local_width)
        shrink_grid = grad_shrink.reshape(model_width, 4, local_width)
        weight_groups[layer_index] = (grad_heads, grad_merge, expand_grid, shrink_grid)
        grad_stream = grad_middle + grad_in_norm
    input_grad = grad_stream.reshape(clip_count, frame_count, model_width)
    heads_grad, merge_grad, expand_grad, shrink_grad = (
        lax.psum_scatter(
            stack_member(weight_groups, 0).astype(jnp.bfloat16),
            ("dp", "seq"),
            scatter_dimension=1,
            tiled=True,
        ).astype(jnp.float32),
        lax.psum_scatter(
            stack_member(weight_groups, 1).astype(jnp.bfloat16),
            ("dp", "seq"),
            scatter_dimension=1,
            tiled=True,
        ).astype(jnp.float32),
        lax.psum_scatter(
            stack_member(weight_groups, 2).astype(jnp.bfloat16),
            ("dp", "seq"),
            scatter_dimension=1,
            tiled=True,
        ).astype(jnp.float32),
        lax.psum_scatter(
            stack_member(weight_groups, 3).astype(jnp.bfloat16),
            ("dp", "seq"),
            scatter_dimension=1,
            tiled=True,
        ).astype(jnp.float32),
    )
    shared_grad, split_grad = (
        lax.psum(jnp.stack(shared_groups).astype(jnp.bfloat16), ("dp", "seq")).astype(jnp.float32),
        lax.psum(jnp.stack(split_groups).astype(jnp.bfloat16), ("dp", "seq")).astype(jnp.float32),
    )
    heads_renewed, heads_updated = adam_update(
        heads_weight, heads_grad, heads_first, heads_second, 0.1
    )
    merge_renewed, merge_updated = adam_update(
        merge_weight, merge_grad, merge_first, merge_second, 0.1
    )
    expand_renewed, expand_updated = adam_update(
        expand_weight, expand_grad, expand_first, expand_second, 0.1
    )
    shrink_renewed, shrink_updated = adam_update(
        shrink_weight, shrink_grad, shrink_first, shrink_second, 0.1
    )
    shared_renewed, shared_updated = adam_update(
        shared_vectors, shared_grad, shared_first, shared_second, 2.0
    )
    split_renewed, split_updated = adam_update(
        split_vectors, split_grad, split_first, split_second, 0.5
    )
    return (
        encoded,
        input_grad,
        heads_grad,
        heads_renewed,
        heads_updated,
        merge_grad,
        merge_renewed,
        merge_updated,
        expand_grad,
        expand_renewed,
        expand_updated,
        shrink_grad,
        shrink_renewed,
        shrink_updated,
        shared_grad,
        shared_renewed,
        shared_updated,
        split_grad,
        split_renewed,
        split_updated,
    )


def solution(mesh):
    placed = (
        P("dp", "seq", None),
        P("dp", "seq", None),
        P(None, ("dp", "seq"), None, "tensor"),
        P(None, ("dp", "seq"), "tensor"),
        P(None, ("dp", "seq"), None, "tensor"),
        P(None, ("dp", "seq"), None, "tensor"),
        P(),
        P(None, None, "tensor"),
        P(None, ("dp", "seq"), None, "tensor"),
        P(None, ("dp", "seq"), None, "tensor"),
        P(None, ("dp", "seq"), "tensor"),
        P(None, ("dp", "seq"), "tensor"),
        P(None, ("dp", "seq"), None, "tensor"),
        P(None, ("dp", "seq"), None, "tensor"),
        P(None, ("dp", "seq"), None, "tensor"),
        P(None, ("dp", "seq"), None, "tensor"),
        P(),
        P(),
        P(None, None, "tensor"),
        P(None, None, "tensor"),
    )
    return jax.shard_map(
        shards,
        mesh=mesh,
        in_specs=placed,
        out_specs=(
            P("dp", "seq", None),
            P("dp", "seq", None),
            P(None, ("dp", "seq"), None, "tensor"),
            P(None, ("dp", "seq"), None, "tensor"),
            P(None, ("dp", "seq"), None, "tensor"),
            P(None, ("dp", "seq"), "tensor"),
            P(None, ("dp", "seq"), "tensor"),
            P(None, ("dp", "seq"), "tensor"),
            P(None, ("dp", "seq"), None, "tensor"),
            P(None, ("dp", "seq"), None, "tensor"),
            P(None, ("dp", "seq"), None, "tensor"),
            P(None, ("dp", "seq"), None, "tensor"),
            P(None, ("dp", "seq"), None, "tensor"),
            P(None, ("dp", "seq"), None, "tensor"),
            P(),
            P(),
            P(),
            P(None, None, "tensor"),
            P(None, None, "tensor"),
            P(None, None, "tensor"),
        ),
        check_vma=False,
    )
```

profile of v0, /device:TPU:10, one launch (start us, length us, event | category | flops | bytes accessed | tf_op | source)
XLA Modules:
  0.0 1034.8 jit_solution(16016935360360867781)
XLA Ops:
  7.3 2.3 copy.202
  13.8 18.8 %all_gather.27 = bf16[2,768,192]{2,1,0:T(8,128)(2,1)S(1)} all-gather(bf16[2,96,192]{2,1,0:T(8,128)(2,1)S(1)} %convert_element_type.225), channel_id=1, replica_groups=mesh['dp'=4,'seq'=2,'tensor'=4] {'dp','seq'}, dimensions={1}, use_global_device_ids=true | all-gather | bytes 663552 | tf_op jit(solution)/shard_map/all_gather | solution.py:117
  34.5 6.9 all-gather.6.cloned.1.call-done
  41.4 8.6 fusion.131
  49.9 5.5 copy.143
  56.4 7.8 all-gather
  64.3 12.0 %all_gather.25 = bf16[1,1024,192]{1,2,0:T(8,128)(2,1)S(1)} all-gather(bf16[1,512,192]{1,2,0:T(8,128)(2,1)S(1)} %fusion.76), channel_id=1, replica_groups=mesh['dp'=4,'seq'=2,'tensor'=4] {'seq'}, dimensions={1}, use_global_device_ids=true | all-gather | bytes 589824 | tf_op jit(solution)/shard_map/all_gather | solution.py:147
  84.6 4.1 fusion.130
  88.7 2.3 copy.144
  91.0 24.5 %all-gather.10.cloned.1.call-done = bf16[2,768,4,192]{3,2,0,1:T(4,128)(2,1)} async-done(((bf16[2,96,4,192]{3,2,0,1:T(4,128)(2,1)}), bf16[2,768,4,192]{3,2,0,1:T(4,128)(2,1)}) %all-gather.10.cloned.1.call-update) | async-done | bytes 2359312 | tf_op jit(solution)/shard_map/all_gather | solution.py:119
  115.5 4.1 fusion.129
  119.6 2.2 copy.145
  121.8 64.8 %all-reduce.10.cloned.1.call-done = f32[512,768]{1,0:T(8,128)} async-done(((f32[512,768]{1,0:T(8,128)}), f32[512,768]{1,0:T(8,128)}) %all-reduce.10.cloned.1.call-update) | async-done | bytes 1572880 | tf_op jit(solution)/shard_map/psum | solution.py:73
  190.1 5.4 multiply_convert_fusion.3
  199.7 6.4 copy.146
  206.2 60.6 %all-reduce.12.cloned.1.call-done = f32[512,768]{1,0:T(8,128)} async-done(((f32[512,768]{1,0:T(8,128)}), f32[512,768]{1,0:T(8,128)}) %all-reduce.12.cloned.1.call-update) | async-done | bytes 1572880 | tf_op jit(solution)/shard_map/psum | solution.py:73
  271.1 7.1 all-gather.1
  278.4 6.3 all_gather.30
  293.9 2.1 copy.147
  296.0 2.7 copy.148
  298.7 63.0 %all-reduce.14.cloned.1.call-done = f32[512,768]{1,0:T(8,128)} async-done(((f32[512,768]{1,0:T(8,128)}), f32[512,768]{1,0:T(8,128)}) %all-reduce.14.cloned.1.call-update) | async-done | bytes 1572880 | tf_op jit(solution)/shard_map/psum | solution.py:73
  365.3 5.1 multiply_convert_fusion.2
  374.8 67.6 %all-reduce.16.cloned.1.call-done = f32[512,768]{1,0:T(8,128)} async-done(((f32[512,768]{1,0:T(8,128)}), f32[512,768]{1,0:T(8,128)}) %all-reduce.16.cloned.1.call-update) | async-done | bytes 1572880 | tf_op jit(solution)/shard_map/psum | solution.py:77
  442.5 3.2 multiply_reduce_fusion.4
  445.7 2.2 fusion.123
  449.3 2.1 multiply_reduce_fusion.1
  455.1 5.2 fusion.6
  460.4 3.4 bitcast_reduce_fusion.1
  463.8 8.8 reduce-scatter.17.cloned.1.call-done
  473.6 19.4 %reduce-scatter.19.cloned.1.call-done = f32[1,512,192]{1,2,0:T(8,128)} async-done(((f32[1,1024,192]{1,2,0:T(8,128)}), f32[1,512,192]{1,2,0:T(8,128)}) %reduce-scatter.19.cloned.1.call-update) | async-done | bytes 393232 | tf_op jit(solution)/shard_map/reduce_scatter | solution.py:252
  494.7 3.3 convolution_bitcast_fusion.1
  498.2 68.2 %all-reduce.18.cloned.1.call-done = f32[512,768]{1,0:T(8,128)} async-done(((f32[512,768]{1,0:T(8,128)}), f32[512,768]{1,0:T(8,128)}) %all-reduce.18.cloned.1.call-update) | async-done | bytes 1572880 | tf_op jit(solution)/shard_map/psum | solution.py:77
  566.4 2.7 multiply_reduce_fusion.5
  578.3 68.2 %all-reduce.20.cloned.1.call-done = f32[512,768]{1,0:T(8,128)} async-done(((f32[512,768]{1,0:T(8,128)}), f32[512,768]{1,0:T(8,128)}) %all-reduce.20.cloned.1.call-update) | async-done | bytes 1572880 | tf_op jit(solution)/shard_map/psum | solution.py:77
  646.6 2.8 multiply_reduce_fusion.6
  649.4 2.1 fusion.121
  659.4 5.0 fusion.4
  664.5 2.4 fusion.47
  668.2 2.3 copy.137
  672.0 3.0 convolution_convert_fusion
  675.0 3.7 copy.114
  678.8 3.0 convolution_convert_fusion.1
  681.8 3.7 copy.113
  685.5 4.7 copy_bitcast_fusion
  690.2 6.9 reshape.492
  698.5 3.1 convolution_convert_fusion.2
  701.7 3.6 copy.112
  705.3 3.1 convolution_convert_fusion.3
  708.5 3.7 copy.111
  712.2 4.6 copy_bitcast_fusion.1
  716.8 6.9 reshape.490
  734.8 5.9 copy.135
  740.7 7.0 reshape.486
  749.0 3.2 fusion.135
  760.8 2.1 copy.103
  780.5 2.1 multiply_subtract_fusion.3
  788.4 38.6 %reduce-scatter.29.cloned.1.call-done = bf16[96,1536]{1,0:T(8,128)(2,1)} async-done(((bf16[768,1536]{1,0:T(8,128)(2,1)}), bf16[96,1536]{1,0:T(8,128)(2,1)}) %reduce-scatter.29.cloned.1.call-update) | async-done | bytes 294928
  829.1 5.6 multiply_subtract_fusion
  834.7 35.0 %reduce-scatter.25.cloned.1.call-done = bf16[96,1152]{1,0:T(8,128)(2,1)} async-done(((bf16[768,1152]{1,0:T(8,128)(2,1)}), bf16[96,1152]{1,0:T(8,128)(2,1)}) %reduce-scatter.25.cloned.1.call-update) | async-done | bytes 221200
  874.0 2.7 multiply_subtract_fusion.2
  876.7 2.2 copy.124
  880.0 112.1 %all-reduce.22.cloned.1.call-done = (f32[512,768]{1,0:T(8,128)}, f32[512,768]{1,0:T(8,128)}) async-done(((f32[512,768]{1,0:T(8,128)}, f32[512,768]{1,0:T(8,128)}), (f32[512,768]{1,0:T(8,128)}, f32[512,768]{1,0:T(8,128)})) %all-reduce.22.cloned.1.call-update) | async-done | bytes 3145744 | tf_op jit(solution)/shard_map/psum | solution.py:77
  995.2 23.9 %all-reduce.1 = (bf16[2,6,768]{2,1,0:T(8,128)(2,1)S(1)}, bf16[2,6,192]{2,1,0:T(8,128)(2,1)S(1)}) all-reduce(bf16[2,6,768]{2,1,0:T(8,128)(2,1)S(1)} %pad_maximum_fusion.6, bf16[2,6,192]{2,1,0:T(8,128)(2,1)S(1)} %pad_maximum_fusion.7), channel_id=1, replica_groups=mesh['dp'=4,'seq'=2,'tensor'=4] {'dp','seq'}, use_global_device_ids=true, to_apply=%region_50.51 | all-reduce | flops 11520 | bytes 46080 | tf_op jit(solution)/shard_map/psum | solution.py:327
  1022.9 4.6 add_bitcast_fusion
  (517 shorter events, 131.5 us)
Async XLA Ops:
  7.2 34.1 %all-gather.6.cloned.1.call-start = ((), (), s32[]{:S(2)}) async-start(), calls=%async_computation.8 | async-start | bytes 2654208 | tf_op jit(solution)/shard_map/all_gather | solution.py:116
  9.6 74.9 %all-gather.8.cloned.1.call-start = ((), (), s32[]{:S(2)}) async-start(), calls=%async_computation.10 | async-start | bytes 3538944 | tf_op jit(solution)/shard_map/all_gather | solution.py:118
  10.6 22.0 %copy-start.81 = (f32[2,6,768]{2,0,1:T(2,128)S(1)}, f32[2,6,768]{2,0,1:T(2,128)}, u32[]{:S(2)}) copy-start(f32[2,6,768]{2,0,1:T(2,128)} %param.26) | copy-start | bytes 110596
  10.6 104.9 %all-gather.10.cloned.1.call-start = ((), (), s32[]{:S(2)}) async-start(), calls=%async_computation.11 | async-start | bytes 3538944 | tf_op jit(solution)/shard_map/all_gather | solution.py:119
  11.6 175.0 %all-reduce.10.cloned.1.call-start = ((), (), s32[]{:S(2)}) async-start(), calls=%async_computation.9 | async-start | bytes 3145728 | tf_op jit(solution)/shard_map/psum | solution.py:73
  11.8 43.6 %copy-start.87 = (f32[512]{0:T(512)}, f32[512]{0:T(512)S(1)}, u32[]{:S(2)}) copy-start(f32[512]{0:T(512)S(1)} %broadcast_multiply_fusion.3) | copy-start | bytes 6148
  32.6 49.4 %copy-start.27 = (bf16[2,768,192]{2,1,0:T(8,128)(2,1)}, bf16[2,768,192]{2,1,0:T(8,128)(2,1)S(1)}, u32[]{:S(2)}) copy-start(bf16[2,768,192]{2,1,0:T(8,128)(2,1)S(1)} %all_gather.27) | copy-start | bytes 1769476
  33.4 22.0 %copy-start.85 = (f32[768]{0:T(1024)}, f32[768]{0:T(1024)S(1)}, u32[]{:S(2)}) copy-start(f32[768]{0:T(1024)S(1)} %get-tuple-element.194) | copy-start | bytes 9220
  33.4 22.0 %copy-start.154 = (f32[768]{0:T(1024)}, f32[768]{0:T(1024)S(1)}, u32[]{:S(2)}) copy-start(f32[768]{0:T(1024)S(1)} %get-tuple-element.193) | copy-start | bytes 9220
  33.4 155.2 %copy-start.97 = (f32[768]{0:T(1024)}, f32[768]{0:T(1024)S(1)}, u32[]{:S(2)}) copy-start(f32[768]{0:T(1024)S(1)} %get-tuple-element.191) | copy-start | bytes 9220
  33.4 235.9 %copy-start.94 = (f32[768]{0:T(1024)}, f32[768]{0:T(1024)S(1)}, u32[]{:S(2)}) copy-start(f32[768]{0:T(1024)S(1)} %get-tuple-element.188) | copy-start | bytes 9220
  34.5 15.4 %copy-start.121 = (f32[512]{0:T(512)}, f32[512]{0:T(512)S(1)}, u32[]{:S(2)}) copy-start(f32[512]{0:T(512)S(1)} %fusion.25) | copy-start | bytes 6148
  34.5 20.9 %copy-start.127 = (f32[512]{0:T(512)}, f32[512]{0:T(512)S(1)}, u32[]{:S(2)}) copy-start(f32[512]{0:T(512)S(1)} %fusion.103) | copy-start | bytes 6148
  56.3 19.9 %copy-start.117 = (f32[3,64]{1,0:T(4,128)S(1)}, f32[3,64]{1,0:T(4,128)}, u32[]{:S(2)}) copy-start(f32[3,64]{1,0:T(4,128)} %add.382) | copy-start | bytes 2308
  56.4 21.1 %copy-start.36 = (f32[512,1,192]{0,2,1:T(8,128)}, f32[512,1,192]{0,2,1:T(8,128)S(1)}, u32[]{:S(2)}) copy-start(f32[512,1,192]{0,2,1:T(8,128)S(1)} %slice.190) | copy-start | bytes 1179652
  83.6 183.2 %all-reduce.12.cloned.1.call-start = ((), (), s32[]{:S(2)}) async-start(), calls=%async_computation.12 | async-start | bytes 3145728 | tf_op jit(solution)/shard_map/psum | solution.py:73
  119.6 67.0 %copy-start.142 = (f32[768]{0:T(1024)S(1)}, f32[768]{0:T(1024)}, u32[]{:S(2)}) copy-start(f32[768]{0:T(1024)} %get-tuple-element.192) | copy-start | bytes 9220
  188.3 78.5 %copy-start.5 = (f32[512,768]{1,0:T(8,128)}, f32[512,768]{1,0:T(8,128)S(1)}, u32[]{:S(2)}) copy-start(f32[512,768]{1,0:T(8,128)S(1)} %get-tuple-element.228) | copy-start | bytes 4718596
  198.4 163.3 %all-reduce.14.cloned.1.call-start = ((), (), s32[]{:S(2)}) async-start(), calls=%async_computation.13 | async-start | bytes 3145728 | tf_op jit(solution)/shard_map/psum | solution.py:73
  199.7 67.0 %copy-start.140 = (f32[768]{0:T(1024)S(1)}, f32[768]{0:T(1024)}, u32[]{:S(2)}) copy-start(f32[768]{0:T(1024)} %get-tuple-element.189) | copy-start | bytes 9220
  268.4 93.3 %copy-start.7 = (f32[512,768]{1,0:T(8,128)}, f32[512,768]{1,0:T(8,128)S(1)}, u32[]{:S(2)}) copy-start(f32[512,768]{1,0:T(8,128)S(1)} %get-tuple-element.224) | copy-start | bytes 4718596
  271.1 14.8 %copy-start.38 = (f32[512,1,192]{0,2,1:T(8,128)}, f32[512,1,192]{0,2,1:T(8,128)S(1)}, u32[]{:S(2)}) copy-start(f32[512,1,192]{0,2,1:T(8,128)S(1)} %slice.197) | copy-start | bytes 1179652
  292.7 149.7 %all-reduce.16.cloned.1.call-start = ((), (), s32[]{:S(2)}) async-start(), calls=%async_computation.14 | async-start | bytes 3145728 | tf_op jit(solution)/shard_map/psum | solution.py:77
  296.0 65.7 %copy-start.139 = (f32[768]{0:T(1024)S(1)}, f32[768]{0:T(1024)}, u32[]{:S(2)}) copy-start(f32[768]{0:T(1024)} %get-tuple-element.186) | copy-start | bytes 9220
  298.7 71.7 %copy-start.54 = (bf16[1,768,4,192]{1,3,2,0:T(8,128)(2,1)}, bf16[1,768,4,192]{1,3,2,0:T(8,128)(2,1)S(1)}, u32[]{:S(2)}) copy-start(bf16[1,768,4,192]{1,3,2,0:T(8,128)(2,1)S(1)} %copy.148) | copy-start | bytes 3538948
  363.5 82.2 %copy-start.115 = (f32[512]{0:T(512)}, f32[512]{0:T(512)S(1)}, u32[]{:S(2)}) copy-start(f32[512]{0:T(512)S(1)} %broadcast_multiply_fusion) | copy-start | bytes 6148
  363.8 81.9 %copy-start.136 = (f32[512]{0:T(512)}, f32[512]{0:T(512)S(1)}, u32[]{:S(2)}) copy-start(f32[512]{0:T(512)S(1)} %fusion.106) | copy-start | bytes 6148
  374.1 75.0 %slice-start.2 = ((s8[6291456]{0:T(1024)(128)(4,1)}), s8[2097152]{0:T(1024)(128)(4,1)S(1)}, s32[]{:S(2)}) async-start(s8[6291456]{0:T(1024)(128)(4,1)} %bitcast.236), calls=%async_computation.28 | async-start | bytes 4194304
  374.1 98.4 %reduce-scatter.17.cloned.1.call-start = ((), (), s32[]{:S(2)}) async-start(), calls=%async_computation.15 | async-start | bytes 1179648 | tf_op jit(solution)/shard_map/reduce_scatter | solution.py:246
  455.1 37.9 %reduce-scatter.19.cloned.1.call-start = ((), (), s32[]{:S(2)}) async-start(), calls=%async_computation.16 | async-start | bytes 1179648 | tf_op jit(solution)/shard_map/reduce_scatter | solution.py:252
  460.3 106.1 %all-reduce.18.cloned.1.call-start = ((), (), s32[]{:S(2)}) async-start(), calls=%async_computation.17 | async-start | bytes 3145728 | tf_op jit(solution)/shard_map/psum | solution.py:77
  473.6 20.4 %copy-start.71 = (bf16[512,1,192]{0,2,1:T(8,128)(2,1)}, bf16[512,1,192]{0,2,1:T(8,128)(2,1)S(1)}, u32[]{:S(2)}) copy-start(bf16[512,1,192]{0,2,1:T(8,128)(2,1)S(1)} %convert_bitcast_fusion.4) | copy-start | bytes 589828
  494.7 71.7 %copy-start.95 = (f32[768]{0:T(1024)S(1)}, f32[768]{0:T(1024)}, u32[]{:S(2)}) copy-start(f32[768]{0:T(1024)} %copy-done.94) | copy-start | bytes 9220
  494.7 71.7 %copy-start.134 = (f32[512]{0:T(512)S(1)}, f32[512]{0:T(512)}, u32[]{:S(2)}) copy-start(f32[512]{0:T(512)} %copy-done.133) | copy-start | bytes 6148
  497.9 68.5 %copy-start.8 = (f32[512,768]{1,0:T(8,128)S(1)}, f32[512,768]{1,0:T(8,128)}, u32[]{:S(2)}) copy-start(f32[512,768]{1,0:T(8,128)} %copy-done.7) | copy-start | bytes 4718596
  497.9 68.5 %copy-start.113 = (f32[512]{0:T(512)S(1)}, f32[512]{0:T(512)}, u32[]{:S(2)}) copy-start(f32[512]{0:T(512)} %copy-done.112) | copy-start | bytes 6148
  497.9 71.2 %copy-start.126 = (f32[512]{0:T(512)S(1)}, f32[512]{0:T(512)}, u32[]{:S(2)}) copy-start(f32[512]{0:T(512)} %copy-done.125) | copy-start | bytes 6148
  497.9 148.6 %all-reduce.20.cloned.1.call-start = ((), (), s32[]{:S(2)}) async-start(), calls=%async_computation.18 | async-start | bytes 3145728 | tf_op jit(solution)/shard_map/psum | solution.py:77
  578.2 68.4 %copy-start.6 = (f32[512,768]{1,0:T(8,128)S(1)}, f32[512,768]{1,0:T(8,128)}, u32[]{:S(2)}) copy-start(f32[512,768]{1,0:T(8,128)} %copy-done.5) | copy-start | bytes 4718596
  578.2 68.4 %copy-start.98 = (f32[768]{0:T(1024)S(1)}, f32[768]{0:T(1024)}, u32[]{:S(2)}) copy-start(f32[768]{0:T(1024)} %copy-done.97) | copy-start | bytes 9220
  578.2 68.4 %copy-start.110 = (f32[512]{0:T(512)S(1)}, f32[512]{0:T(512)}, u32[]{:S(2)}) copy-start(f32[512]{0:T(512)} %copy-done.109) | copy-start | bytes 6148
  578.2 68.4 %copy-start.131 = (f32[512]{0:T(512)S(1)}, f32[512]{0:T(512)}, u32[]{:S(2)}) copy-start(f32[512]{0:T(512)} %copy-done.130) | copy-start | bytes 6148
  578.3 151.1 %reduce-scatter.21.cloned.1.call-start = ((), (), s32[]{:S(2)}) async-start(), calls=%async_computation.19 | async-start | bytes 1179648 | tf_op jit(solution)/shard_map/reduce_scatter | solution.py:246
  578.3 71.0 %copy-start.124 = (f32[512]{0:T(512)S(1)}, f32[512]{0:T(512)}, u32[]{:S(2)}) copy-start(f32[512]{0:T(512)} %copy-done.123) | copy-start | bytes 6148
  652.4 14.6 %copy-start.16 = (f32[512,768]{1,0:T(8,128)}, f32[512,768]{1,0:T(8,128)S(1)}, u32[]{:S(2)}) copy-start(f32[512,768]{1,0:T(8,128)S(1)} %get-tuple-element.206) | copy-start | bytes 4718596
  659.4 71.2 %reduce-scatter.23.cloned.1.call-start = ((), (), s32[]{:S(2)}) async-start(), calls=%async_computation.20 | async-start | bytes 1179648 | tf_op jit(solution)/shard_map/reduce_scatter | solution.py:252
  664.5 113.5 %reduce-scatter.27.cloned.1.call-start = ((), (), s32[]{:S(2)}) async-start(), calls=%async_computation.22 | async-start | bytes 663552
  671.8 115.2 %reduce-scatter.31.cloned.1.call-start = ((), (), s32[]{:S(2)}) async-start(), calls=%async_computation.24 | async-start | bytes 2654208
  697.2 129.8 %reduce-scatter.29.cloned.1.call-start = ((), (), s32[]{:S(2)}) async-start(), calls=%async_computation.23 | async-start | bytes 2654208
  723.8 145.9 %reduce-scatter.25.cloned.1.call-start = ((), (), s32[]{:S(2)}) async-start(), calls=%async_computation.21 | async-start | bytes 1990656
  747.7 244.4 %all-reduce.22.cloned.1.call-start = ((), (), s32[]{:S(2)}) async-start(), calls=%async_computation.25 | async-start | bytes 6291456 | tf_op jit(solution)/shard_map/psum | solution.py:77
  764.0 22.1 %copy-start.53 = (f32[1,512,192]{1,2,0:T(8,128)S(1)}, f32[1,512,192]{1,2,0:T(8,128)}, u32[]{:S(2)}) copy-start(f32[1,512,192]{1,2,0:T(8,128)} %reduce-scatter.23.cloned.1.call-done) | copy-start | bytes 1179652
  771.4 14.8 %copy-start.150 = (bf16[4,192]{1,0:T(4,128)(2,1)S(1)}, bf16[4,192]{1,0:T(4,128)(2,1)}, u32[]{:S(2)}) copy-start(bf16[4,192]{1,0:T(4,128)(2,1)} %reshape.466) | copy-start | bytes 4612
  780.5 48.6 %copy-start.41 = (f32[2,96,4,192]{3,2,1,0:T(4,128)S(1)}, f32[2,96,4,192]{3,2,1,0:T(4,128)}, u32[]{:S(2)}) copy-start(f32[2,96,4,192]{3,2,1,0:T(4,128)} %param.24) | copy-start | bytes 1769476
  834.6 39.3 %copy-start.43 = (f32[2,96,3,192]{1,3,2,0:T(8,128)S(1)}, f32[2,96,3,192]{1,3,2,0:T(8,128)}, u32[]{:S(2)}) copy-start(f32[2,96,3,192]{1,3,2,0:T(8,128)} %copy.106) | copy-start | bytes 1327108
  878.9 115.3 %copy-start.122 = (f32[512]{0:T(512)S(1)}, f32[512]{0:T(512)}, u32[]{:S(2)}) copy-start(f32[512]{0:T(512)} %copy-done.121) | copy-start | bytes 6148
  878.9 115.3 %copy-start.129 = (f32[512]{0:T(512)S(1)}, f32[512]{0:T(512)}, u32[]{:S(2)}) copy-start(f32[512]{0:T(512)} %copy-done.127) | copy-start | bytes 6148
  994.1 25.6 %copy-start.82 = (f32[2,6,768]{2,0,1:T(2,128)S(1)}, f32[2,6,768]{2,0,1:T(2,128)}, u32[]{:S(2)}) copy-start(f32[2,6,768]{2,0,1:T(2,128)} %param.26) | copy-start | bytes 110596
  994.1 25.6 %copy-start.92 = (f32[2,6,768]{2,0,1:T(2,128)S(1)}, f32[2,6,768]{2,0,1:T(2,128)}, u32[]{:S(2)}) copy-start(f32[2,6,768]{2,0,1:T(2,128)} %param.36) | copy-start | bytes 110596
  994.1 25.6 %copy-start.93 = (f32[2,6,768]{2,0,1:T(2,128)S(1)}, f32[2,6,768]{2,0,1:T(2,128)}, u32[]{:S(2)}) copy-start(f32[2,6,768]{2,0,1:T(2,128)} %param.37) | copy-start | bytes 110596
  994.1 27.5 %copy-start.90 = (f32[2,6,192]{2,0,1:T(2,128)S(1)}, f32[2,6,192]{2,0,1:T(2,128)}, u32[]{:S(2)}) copy-start(f32[2,6,192]{2,0,1:T(2,128)} %param.27) | copy-start | bytes 27652
  994.1 27.5 %copy-start.143 = (f32[2,6,192]{2,0,1:T(2,128)S(1)}, f32[2,6,192]{2,0,1:T(2,128)}, u32[]{:S(2)}) copy-start(f32[2,6,192]{2,0,1:T(2,128)} %param.38) | copy-start | bytes 27652
  994.1 27.5 %copy-start.144 = (f32[2,6,192]{2,0,1:T(2,128)S(1)}, f32[2,6,192]{2,0,1:T(2,128)}, u32[]{:S(2)}) copy-start(f32[2,6,192]{2,0,1:T(2,128)} %param.39) | copy-start | bytes 27652
  994.2 28.7 %copy-start.138 = (f32[768]{0:T(1024)S(1)}, f32[768]{0:T(1024)}, u32[]{:S(2)}) copy-start(f32[768]{0:T(1024)} %get-tuple-element.183) | copy-start | bytes 9220
  (124 other events, 343.2 us)
Sparse Core Ops, SparseCore 0:
  10.5 30.8 all-gather.5
  43.8 36.8 all-gather.7
  83.1 32.3 all-gather.9
  118.3 68.2 all-reduce.9
  198.5 68.1 all-reduce.11
  292.9 68.8 all-reduce.13
  374.3 68.1 all-reduce.15
  455.2 17.3 reduce-scatter.16
  475.5 17.4 reduce-scatter.18
  498.1 68.2 all-reduce.17
  578.4 68.1 all-reduce.19
  659.5 17.3 reduce-scatter.20
  679.7 17.4 reduce-scatter.22
  700.8 34.3 reduce-scatter.26
  738.4 42.5 reduce-scatter.30
  784.5 42.4 reduce-scatter.28
  830.2 39.4 reduce-scatter.24
  872.5 119.5 all-reduce.21
where the time goes:
time: 1050 us; the launch traced here: 1030 us
  waiting for transfers between devices  638 us (61%)
  local copies, waits for them, and re-layouts  156 us (15%)
  matrix products  81.5 us (8%)
  blocking collectives  75.9 us (7%)
  other arithmetic  64.5 us (6%)
  between operations  16.5 us (2%)
    psum x4, waiting for transfers between devices, back_total(): return lax.psum(partial_sum, 'tensor')  316 us
    psum x3, waiting for transfers between devices, head_total(): return lax.psum(partial_sum, 'tensor')  188 us
    unnamed x379, local copies, waits for them, and re-layouts  105 us
    unnamed x22, waiting for transfers between devices  73.9 us
    all_gather x1, waiting for transfers between devices, shards(): lax.all_gather(shrink_weight.astype(jnp.bfloat16), ('dp', 'seq'), axis=1,...  24.5 us
    psum x1, blocking collectives, shards(): lax.psum(jnp.stack(shared_groups).astype(jnp.bfloat16), ('dp', 'seq'))  23.9 us
  transfers between devices with their start and end apart: 18, of which 13 were waited for; matrix products, arithmetic and copies ran while one was open for 20% of the time, Pallas kernels for 0%

commit v1 on v0

v1 whole, which is shorter than its diff:
```python
import math

import jax
import jax.numpy as jnp
from jax import lax
from jax.experimental import pallas as pl
from jax.experimental.pallas import tpu as pltpu
from jax.sharding import PartitionSpec as P

HEAD_DIM = 64
STEP = 10

beta_one = 0.9
beta_two = 0.999
adam_epsilon = 1e-08
weight_decay = 0.01
norm_epsilon = 1e-05

MESH = pl.DeviceIdType.MESH
F32 = jnp.float32
BF16 = jnp.bfloat16


def dot(a, b):
    return lax.dot_general(a, b, (((1,), (0,)), ((), ())), preferred_element_type=F32)


def dot_nt(a, b):
    return lax.dot_general(a, b, (((1,), (1,)), ((), ())), preferred_element_type=F32)


def dot_tn(a, b):
    return lax.dot_general(a, b, (((0,), (0,)), ((), ())), preferred_element_type=F32)


def norm_parts(values):
    centre = values - jnp.mean(values, axis=-1, keepdims=True)
    spread = jnp.mean(centre * centre, axis=-1, keepdims=True)
    inverse = lax.rsqrt(spread + norm_epsilon)
    return centre * inverse, inverse


def norm_back(grad, hat, inverse, gain):
    scaled = grad * gain
    first = jnp.mean(scaled, axis=-1, keepdims=True)
    second = jnp.mean(scaled * hat, axis=-1, keepdims=True)
    return inverse * (scaled - first - hat * second)


class Numbers:
    def __init__(self):
        self.count = 0

    def take(self, n):
        base = self.count
        self.count += n
        return base


def make_kernel(layers, tokens, width, numbers):
    shard = tokens // 4
    rows_of = 96
    take = numbers.take
    rs_base = [take(3) for _ in range(3 * layers)]
    ag_base = [take(4) for _ in range(4 * layers)]
    sp_base = [take(16), take(16)]
    sv_base, sz_base, sc_base, sq_base = take(3), take(3), take(1), take(3)
    cx_base = [take(3) for _ in range(layers)]
    gc_base = [take(3) for _ in range(layers)]
    ob, oa, oc = ([take(n) for _ in range(layers)] for n in (3, 3, 4))
    goc, goa, gob = ([take(n) for _ in range(layers)] for n in (1, 3, 3))
    kv_base = [take(2) for _ in range(layers)]
    gkv_base = [take(1) for _ in range(layers)]
    ab, aa, ac = ([take(n) for _ in range(layers)] for n in (4, 3, 4))
    ma, mb, mc = ([take(n) for _ in range(layers)] for n in (3, 4, 4))
    gac, gaa, gab = ([take(n) for _ in range(layers)] for n in (1, 3, 4))
    gmc, gmb, gma = ([take(n) for _ in range(layers)] for n in (1, 4, 3))
    oz = [take(4) for _ in range(2)]
    op = [take(4) for _ in range(2)]
    top = layers - 1

    def kernel(
        frames, cot, hw, mw, wm, shared, sv,
        enc, xg, gh_out, go_out, gm_out, shared_out, split_out,
        XS, MS, A, N, GO, GY, GS,
        WA, WO, W1, W2, GA, GB, GM,
        QC, KV, VT, E01, E2, RR, CS, CX, CF, GC, H, DG, GF, GQ, G,
        GKV, KVS, KVR,
        OWN, RSS, RSR,
        CM, BM, TM, UM,
        FM, FA, SA, CA, RA, RB, SO, CO, RO, TO, RP,
        EZ, SV, BQ, B1, SMALL, SZ, SC, SP,
        ssem, rsem, lsem,
    ):
        dp = lax.axis_index("dp")
        y = lax.axis_index("seq")
        z = lax.axis_index("tensor")
        hi = lax.div(dp, 4)
        lo = lax.rem(dp, 4)
        xx = lax.div(lo, 2)
        cc = lax.rem(lo, 2)
        t = 2 * xx + y

        def flip(bit, by):
            return bit + by - 2 * bit * by

        def peer(k):
            if isinstance(k, int):
                kx, ky = k // 2, k % 2
            else:
                kx, ky = lax.div(k, 2), lax.rem(k, 2)
            return flip(xx, kx), flip(y, ky)

        def peer_t(k):
            px, py = peer(k)
            return 2 * px + py

        def peer_dev(k):
            px, py = peer(k)
            return {"dp": 4 * hi + 2 * px + cc, "seq": py}

        def peer_j(k):
            px, py = peer(k)
            return 4 * px + 2 * cc + py

        my_j = 4 * xx + 2 * cc + y
        sib = {"dp": dp + 1 - 2 * cc}

        def z_to(k):
            return lax.rem(z + k, 4)

        def z_from(k):
            return lax.rem(z + 4 - k, 4)

        middle = jnp.logical_or(z == 1, z == 2)

        def z_near(k, act):
            if k == 2:
                act()
            else:
                pl.when(z != (3 if k == 1 else 0))(act)

        def z_far(k, act):
            pl.when(z == (3 if k == 1 else 0))(act)

        def z_come(k, act):
            pl.when(z != (0 if k == 1 else 3))(act)

        def gather_z(slot, base):
            def copy(k):
                return remote(slot(z), slot(z), base + k - 1, {"tensor": z_to(k)})

            def relay():
                far = slot(z_from(2))
                return remote(
                    far, far, base + 2 * (z - 1), {"tensor": 3 * (z - 1)}, send=base + 3
                )

            def wait(k):
                remote(slot(z), slot(z_from(k)), base + k - 1, sib).wait_recv()

            def start():
                for k in (2, 1, 3):
                    z_near(k, lambda k=k: copy(k).start())

            def pass_on():
                wait(2)
                pl.when(middle)(lambda: relay().start())

            def drain():
                for k in (2, 1, 3):
                    z_near(k, lambda k=k: copy(k).wait_send())
                pl.when(middle)(lambda: relay().wait_send())

            return start, pass_on, wait, drain

        def sum_z(part, far, landing, base):
            def copy(k):
                return remote(part(z_to(k)), landing(k), base + k - 1, {"tensor": z_to(k)})

            def far_copy():
                end = lax.div(z, 3)
                return remote(part(3 - z), far, base + 3, {"tensor": 1 + end})

            def start_far():
                pl.when(jnp.logical_not(middle))(lambda: far_copy().start())

            def start():
                for k in (1, 3):
                    z_near(k, lambda k=k: copy(k).start())
                    at = landing(k)

                    @pl.when(z == (0 if k == 1 else 3))
                    def _(at=at):
                        at[...] = jnp.zeros(at.shape, BF16)

                pl.when(jnp.logical_not(middle))(lambda: copy(2).start())

            def combine():
                @pl.when(middle)
                def _():
                    far_copy().wait_recv()
                    at = part(z_to(2))
                    at[...] = (at[...].astype(F32) + far[...].astype(F32)).astype(BF16)
                    copy(2).start()

            def wait():
                copy(2).wait_recv()
                for k in (1, 3):
                    z_come(k, lambda k=k: copy(k).wait_recv())

            def drain():
                copy(2).wait_send()
                for k in (1, 3):
                    z_near(k, lambda k=k: copy(k).wait_send())
                pl.when(jnp.logical_not(middle))(lambda: far_copy().wait_send())

            return start, combine, wait, drain, start_far

        def remote(src, dst, number, dev, send=None):
            send = number if send is None else send
            return pltpu.make_async_remote_copy(
                src_ref=src,
                dst_ref=dst,
                send_sem=ssem.at[send],
                recv_sem=rsem.at[number],
                device_id=dev,
                device_id_type=MESH,
            )

        def rows(k_t):
            return pl.ds(pl.multiple_of(k_t * shard, shard), shard)

        def block(j):
            return pl.ds(pl.multiple_of(j * rows_of, rows_of), rows_of)

        X0 = GF
        lower = lax.broadcasted_iota(jnp.int32, (1, 128), 1) < 64
        top_rows = lax.broadcasted_iota(jnp.int32, (128, 1), 0) < 64

        barrier = pltpu.get_barrier_semaphore()
        for k in range(1, 8):
            dev = {
                "dp": 4 * hi + 2 * flip(xx, k // 4) + flip(cc, (k // 2) % 2),
                "seq": flip(y, k % 2),
            }
            pl.semaphore_signal(barrier, inc=1, device_id=dev, device_id_type=MESH)
        for k in range(1, 4):
            pl.semaphore_signal(
                barrier, inc=1, device_id={"tensor": z_to(k)}, device_id_type=MESH
            )
        pl.semaphore_wait(barrier, 10)

        xs = lax.div(z, 2)
        source = jnp.logical_and(lo == z, y == cc)
        relay = jnp.logical_and(xx != xs, y == cc)
        relay_dev = {"dp": dp, "seq": 1 - y}

        def piece(p):
            return pl.ds(p * shard, shard)

        def spread_each(src, dst, i, act, act_own):
            @pl.when(lo == z)
            def _():
                for p in range(4):
                    for d, (dx, dy) in enumerate(((1, 0), (0, 1), (0, 0))):
                        same = jnp.logical_and(cc == y, (dx, dy) == (0, 0))
                        dev = {"dp": 4 * hi + 2 * flip(xx, dx) + y, "seq": flip(y, dy)}

                        @pl.when(jnp.logical_not(same))
                        def _(p=p, d=d, dev=dev):
                            act(
                                remote(
                                    src.at[piece(p)],
                                    dst.at[piece(p)],
                                    sp_base[i] + p,
                                    dev,
                                    send=sp_base[i] + 4 + 3 * p + d,
                                )
                            )

            if act_own is not None:

                @pl.when(source)
                def _():
                    act_own(pltpu.make_async_copy(src, dst, lsem.at[i]))

        def spread_start(src, dst, i):
            spread_each(src, dst, i, lambda c: c.start(), lambda c: c.start())

        def relay_copy(dst, i, p):
            return remote(
                dst.at[piece(p)],
                dst.at[piece(p)],
                sp_base[i] + p,
                relay_dev,
                send=sp_base[i] + 4 + p,
            )

        def spread_pass(dst, i, p):
            @pl.when(relay)
            def _():
                relay_copy(dst, i, p).wait_recv()
                relay_copy(dst, i, p).start()

        def spread_wait(src, dst, i, p):
            if p == 0:

                @pl.when(source)
                def _():
                    pltpu.make_async_copy(src, dst, lsem.at[i]).wait()

            @pl.when(jnp.logical_not(jnp.logical_or(source, relay)))
            def _():
                relay_copy(dst, i, p).wait_recv()

        def spread_drain(src, dst, i):
            spread_each(src, dst, i, lambda c: c.wait_send(), None)

            @pl.when(relay)
            def _():
                for p in range(4):
                    relay_copy(dst, i, p).wait_send()

        att_z = [gather_z(lambda b, l=l: GA.at[l, b], ab[l]) for l in range(layers)]
        mlp_z = [gather_z(lambda b, l=l: GM.at[l, cc, b], mb[l]) for l in range(layers)]
        out_z = [gather_z(lambda b, i=i: EZ.at[i, b], oz[i]) for i in range(2)]

        def att_b_start(l):
            q, k, v = (hw[l, i].astype(BF16) for i in range(3))
            GA[l, z, :, 0:128] = q[:, 0:128]
            GA[l, z, :, 128:256] = jnp.concatenate([q[:, 128:192], k[:, 128:192]], axis=1)
            GA[l, z, :, 256:384] = k[:, 0:128]
            GA[l, z, :, 384:512] = v[:, 0:128]
            third = v[:, 128:192]
            GA[l, z, :, 512:640] = jnp.concatenate([third, jnp.zeros_like(third)], axis=1)
            att_z[l][0]()

        def att_a_copy(l, b):
            bx, by = lax.div(b, 2), lax.rem(b, 2)
            k = 2 * flip(xx, bx) + flip(y, by)
            return remote(
                GA.at[l, b],
                WA.at[l, block(my_j)],
                aa[l] + k - 1,
                {"dp": 4 * hi + 2 * bx + cc, "seq": by},
            )

        def att_a_piece(l, zk):
            b = z_from(zk)

            @pl.when(b != t)
            def _():
                att_a_copy(l, b).start()

            @pl.when(b == t)
            def _():
                WA[l, block(my_j)] = GA[l, t]

        def att_a_first(l):
            att_z[l][1]()
            att_a_piece(l, 2)

        def att_a_rest(l):
            for k in (1, 3):
                att_z[l][2](k)
                att_a_piece(l, k)

        def att_c_copy(l, k):
            at = WA.at[l, block(peer_j(k))]
            return remote(at, at, ac[l] + k, sib)

        def att_c_start(l):
            att_c_copy(l, 0).start()
            for k in range(1, 4):
                remote(
                    GA.at[l, 0], WA.at[l, block(peer_j(k))], aa[l] + k - 1, sib
                ).wait_recv()
                att_c_copy(l, k).start()

        def att_ready(l):
            for k in range(4):
                px, py = peer(k)
                at = WA.at[l, block(4 * px + 2 * (1 - cc) + py)]
                remote(at, at, ac[l] + k, sib).wait_recv()

        def att_drain(l):
            att_z[l][3]()
            for k in range(1, 4):
                att_a_copy(l, peer_t(k)).wait_send()
            for k in range(4):
                att_c_copy(l, k).wait_send()

        def out_b_copy(l, k):
            return remote(GB.at[l, z], GB.at[l, z], ob[l] + k - 1, {"tensor": z_to(k)})

        def out_b_start(l):
            own = mw[l].astype(BF16)
            third = own[:, 128:192]
            none = jnp.zeros_like(third)
            odd = lax.rem(z, 2) == 1
            GB[l, z, :, 0:128] = own[:, 0:128]
            GB[l, z, :, 128:256] = jnp.where(
                odd,
                jnp.concatenate([none, third], axis=1),
                jnp.concatenate([third, none], axis=1),
            )
            for k in range(1, 4):
                out_b_copy(l, k).start()

        def out_a_copy(l, k):
            at = WO.at[l, block(my_j)]
            return remote(at, at, oa[l] + k - 1, peer_dev(k))

        def out_a_start(l):
            for k in range(1, 4):
                remote(GB.at[l, z], GB.at[l, z_from(k)], ob[l] + k - 1, sib).wait_recv()
            at = block(my_j)
            for b in range(4):
                WO[l, at, b * 128 : b * 128 + 128] = GB[l, b, :, 0:128]
            for b in range(2):
                pair = GB[l, 2 * b, :, 128:256] + GB[l, 2 * b + 1, :, 128:256]
                WO[l, at, 512 + b * 128 : 640 + b * 128] = pair
            for k in range(1, 4):
                out_a_copy(l, k).start()

        def out_c_copy(l, k):
            at = WO.at[l, block(peer_j(k))]
            return remote(at, at, oc[l] + k, sib)

        def out_c_start(l):
            out_c_copy(l, 0).start()
            for k in range(1, 4):
                at = WO.at[l, block(peer_j(k))]
                remote(at, at, oa[l] + k - 1, sib).wait_recv()
                out_c_copy(l, k).start()

        def out_ready(l):
            for k in range(4):
                px, py = peer(k)
                at = WO.at[l, block(4 * px + 2 * (1 - cc) + py)]
                remote(at, at, oc[l] + k, sib).wait_recv()

        def out_drain(l):
            for k in range(1, 4):
                out_b_copy(l, k).wait_send()
                out_a_copy(l, k).wait_send()
            for k in range(4):
                out_c_copy(l, k).wait_send()

        def mlp_a_copy(l, k):
            return remote(
                wm.at[l, peer_t(k)], GM.at[l, cc, z, t], ma[l] + k - 1, peer_dev(k)
            )

        def mlp_a_start(l):
            for k in range(1, 4):
                mlp_a_copy(l, k).start()
            GM[l, cc, z, t] = wm[l, t]

        def mlp_b_start(l):
            for k in range(1, 4):
                remote(
                    wm.at[l, 0], GM.at[l, cc, z, peer_t(k)], ma[l] + k - 1, sib
                ).wait_recv()
            mlp_z[l][0]()

        def mlp_pass(l):
            mlp_z[l][1]()

        def mlp_c_copy(l, k):
            at = GM.at[l, cc, z_from(k)]
            return remote(at, at, mc[l] + k, sib)

        def mlp_c_start(l):
            mlp_c_copy(l, 0).start()
            mlp_c_copy(l, 2).start()
            for k in (1, 3):
                mlp_z[l][2](k)
                mlp_c_copy(l, k).start()

        def mlp_ready(l):
            for k in range(4):
                at = GM.at[l, 1 - cc, z_from(k)]
                remote(at, at, mc[l] + k, sib).wait_recv()
            for k in range(4):
                mlp_c_copy(l, k).wait_send()
            for k in range(1, 4):
                mlp_a_copy(l, k).wait_send()
            mlp_z[l][3]()

            def unpack(j, carry):
                jc = lax.rem(lax.div(j, 2), 2)
                jq = 2 * lax.div(j, 4) + lax.rem(j, 2)
                at = block(j)
                mixed = []
                for b in range(4):
                    chunk = GM[l, jc, b, jq]
                    W1[l, at, b * 128 : b * 128 + 128] = chunk[:, 0:128]
                    W2[l, at, b * 128 : b * 128 + 128] = chunk[:, 256:384]
                    mixed.append(chunk[:, 128:256].astype(F32))
                for b in range(2):
                    even, odd = mixed[2 * b], mixed[2 * b + 1]
                    lanes = slice(512 + b * 128, 640 + b * 128)
                    W1[l, at, lanes] = jnp.where(
                        lower, even, pltpu.roll(odd, 64, 1)
                    ).astype(BF16)
                    W2[l, at, lanes] = jnp.where(
                        lower, pltpu.roll(even, 64, 1), odd
                    ).astype(BF16)
                return carry

            lax.fori_loop(0, 8, unpack, 0)

        def rs_copy(i, k):
            return remote(RSS.at[k], RSR.at[i % 2, k - 1], rs_base[i] + k - 1, peer_dev(k))

        def rs_loop(i, order, part):
            def step(s, carry):
                k = order(s)
                partial = part(k)
                RSS[k] = partial.astype(BF16)

                @pl.when(k == 0)
                def _():
                    OWN[...] = partial

                @pl.when(k > 0)
                def _():
                    rs_copy(i, k).start()

                return carry

            lax.fori_loop(0, 4, step, 0)

        def rs_finish(i):
            for k in range(1, 4):
                rs_copy(i, k).wait_recv()
            total = OWN[...]
            for k in range(1, 4):
                total = total + RSR[i % 2, k - 1].astype(F32)
            for k in range(1, 4):
                rs_copy(i, k).wait_send()
            return total

        def ag_copy(i, buf, l, k):
            at = buf.at[l, rows(t)]
            return remote(at, at, ag_base[i] + k - 1, peer_dev(k))

        def ag_half(buf, l, k, upper):
            start = peer_t(k) * shard + upper * (shard // 2)
            return buf.at[l, pl.ds(pl.multiple_of(start, shard // 2), shard // 2)]

        def ag_relay(i, buf, l, k):
            at = ag_half(buf, l, k, k - 1)
            return remote(at, at, ag_base[i] + k + 1, peer_dev(3 - k))

        def ag_start(i, buf, l, value):
            buf[l, rows(t)] = value
            for k in (1, 2):
                ag_copy(i, buf, l, k).start()

        def ag_wait(i, buf, l, k):
            @pl.when(k == 1)
            def _():
                for near in (1, 2):
                    at = buf.at[l, rows(peer_t(near))]
                    remote(at, at, ag_base[i] + near - 1, sib).wait_recv()
                    ag_relay(i, buf, l, near).start()

            @pl.when(k == 3)
            def _():
                for upper in (0, 1):
                    at = ag_half(buf, l, 3, upper)
                    remote(at, at, ag_base[i] + 2 + upper, sib).wait_recv()

        def ag_drain(i, buf, l):
            for k in (1, 2):
                ag_copy(i, buf, l, k).wait_send()
                ag_relay(i, buf, l, k).wait_send()

        def forth(s):
            return s

        def back(s):
            return 3 - s

        def row(l, r):
            return shared[r, l : l + 1, :]

        def out_start(i, value):
            EZ[i, z] = value.astype(BF16)
            out_z[i][0]()

        def out_p_each(i, ks, act_far, act_near):
            for k in ks:
                zs = z_from(k)
                near = jnp.logical_and(lo == zs, y == cc)

                @pl.when(near)
                def _(zs=zs):
                    act_near(
                        pltpu.make_async_copy(
                            EZ.at[i, zs], (enc, xg)[i].at[t], lsem.at[2 + i]
                        )
                    )

                @pl.when(jnp.logical_not(near))
                def _(zs=zs, k=k):
                    act_far(
                        remote(
                            EZ.at[i, zs],
                            (enc, xg)[i].at[t],
                            op[i] + t,
                            {"dp": 4 * hi + zs, "seq": cc},
                            send=op[i] + k,
                        )
                    )

        def out_forward(i, ks):
            for k in ks:
                if k % 2 == 1:
                    out_z[i][2](k)
                out_p_each(i, (k,), lambda c: c.start(), lambda c: c.start())

        def out_finish(i, out):
            for d in range(4):
                mine = jnp.logical_and(t == d, cc == y)

                @pl.when(jnp.logical_not(mine))
                def _(d=d):
                    remote(EZ.at[i, 0], out.at[d], op[i] + d, sib).wait_recv()

            out_p_each(i, range(4), lambda c: c.wait_send(), lambda c: c.wait())
            out_z[i][3]()

        def att_grad_c_copy(l):
            return remote(SA.at[1 - cc], CA, gac[l], sib)

        def att_grad_a_copy(l, k):
            return remote(
                SA.at[cc, peer_t(k)], RA.at[l, t], gaa[l] + k - 1, peer_dev(k)
            )

        att_sum = [
            sum_z(lambda b, l=l: RA.at[l, b], FA.at[l], lambda k, l=l: RB.at[l, k - 1], gab[l])
            for l in range(layers)
        ]
        mlp_sum = [
            sum_z(lambda b, l=l: GM.at[l, cc, b], FM.at[l], lambda k, l=l: BM.at[l, k - 1], gmb[l])
            for l in range(layers)
        ]

        def att_grad_a(l):
            att_grad_c_copy(l).wait_recv()

            def add(q, carry):
                SA[cc, q] = (
                    SA[cc, q].astype(F32) + CA[q].astype(F32)
                ).astype(BF16)
                return carry

            lax.fori_loop(0, 4, add, 0)
            for k in range(1, 4):
                att_grad_a_copy(l, k).start()
            RA[l, t] = SA[cc, t]
            att_grad_c_copy(l).wait_send()

        def att_grad_b(l):
            for k in range(1, 4):
                remote(
                    SA.at[0, 0], RA.at[l, peer_t(k)], gaa[l] + k - 1, sib
                ).wait_recv()
            att_sum[l][4]()
            att_sum[l][0]()
            for k in range(1, 4):
                att_grad_a_copy(l, k).wait_send()

        def att_grad_end(l):
            total = RA[l, z].astype(F32)
            att_sum[l][2]()
            for k in range(1, 4):
                total = total + RB[l, k - 1].astype(F32)
            gh_out[l, 0, :, :] = total[:, 0:192].astype(BF16)
            gh_out[l, 1, :, 0:128] = total[:, 256:384].astype(BF16)
            k2 = pltpu.roll(total[:, 128:256], 64, 1)[:, 0:64]
            gh_out[l, 1, :, 128:192] = k2.astype(BF16)
            gh_out[l, 2, :, :] = total[:, 384:576].astype(BF16)
            att_sum[l][3]()

        def out_grad_c_copy(l):
            return remote(SO.at[1 - cc], CO, goc[l], sib)

        def out_grad_a_copy(l, k):
            return remote(SO.at[cc, peer_t(k)], RO.at[l, k - 1], goa[l] + k - 1, peer_dev(k))

        def out_grad_b_copy(l, k):
            return remote(
                TO.at[z_to(k)], RP.at[l, k - 1], gob[l] + k - 1, {"tensor": z_to(k)}
            )

        def out_grads(l):
            def product(b, carry):
                lanes = pl.ds(pl.multiple_of(b * 128, 128), 128)
                W2[l, lanes, :] = dot_tn(GO[l, :, lanes], CF[l]).astype(BF16)
                return carry

            lax.fori_loop(0, 6, product, 0)

            def pack(j, carry):
                jc = lax.rem(lax.div(j, 2), 2)
                jq = 2 * lax.div(j, 4) + lax.rem(j, 2)
                SO[jc, jq] = W2[l, block(j), :]
                return carry

            lax.fori_loop(0, 8, pack, 0)
            out_grad_c_copy(l).start()

        def out_grad_a(l):
            out_grad_c_copy(l).wait_recv()

            def add(q, carry):
                SO[cc, q] = (SO[cc, q].astype(F32) + CO[q].astype(F32)).astype(BF16)
                return carry

            lax.fori_loop(0, 4, add, 0)
            for k in range(1, 4):
                out_grad_a_copy(l, k).start()
            out_grad_c_copy(l).wait_send()

        def out_grad_b(l):
            total = SO[cc, t].astype(F32)
            for k in range(1, 4):
                out_grad_a_copy(l, k).wait_recv()
                total = total + RO[l, k - 1].astype(F32)
            total = total.astype(BF16)
            for b in range(4):
                TO[b, :, 0:128] = total[:, b * 128 : b * 128 + 128]
                pair = 512 + (b // 2) * 128
                TO[b, :, 128:256] = total[:, pair : pair + 128]
            for k in range(1, 4):
                out_grad_b_copy(l, k).start()
            for k in range(1, 4):
                out_grad_a_copy(l, k).wait_send()

        def out_grad_end(l):
            total = TO[z].astype(F32)
            for k in range(1, 4):
                out_grad_b_copy(l, k).wait_recv()
                total = total + RP[l, k - 1].astype(F32)
            go_out[l, :, 0:128] = total[:, 0:128].astype(BF16)
            pair = total[:, 128:256]
            pair = jnp.where(lax.rem(z, 2) == 1, pltpu.roll(pair, 64, 1), pair)
            go_out[l, :, 128:192] = pair[:, 0:64].astype(BF16)
            for k in range(1, 4):
                out_grad_b_copy(l, k).wait_send()

        def mlp_grad_c_copy(l):
            return remote(GM.at[l, 1 - cc], CM, gmc[l], sib)

        def mlp_grad_a_copy(l, k):
            return remote(TM.at[peer_t(k)], UM.at[l, t], gma[l] + k - 1, peer_dev(k))

        def mlp_grad_b(l):
            mlp_grad_c_copy(l).wait_recv()

            def add(s, carry):
                zs, q = lax.div(s, 4), lax.rem(s, 4)
                GM[l, cc, zs, q] = (
                    GM[l, cc, zs, q].astype(F32) + CM[zs, q].astype(F32)
                ).astype(BF16)
                return carry

            lax.fori_loop(0, 16, add, 0)
            mlp_sum[l][4]()
            mlp_grad_c_copy(l).wait_send()

        def mlp_grad_a(l):
            mlp_sum[l][2]()
            for q in range(4):
                total = GM[l, cc, z, q].astype(F32)
                for k in range(1, 4):
                    total = total + BM[l, k - 1, q].astype(F32)
                TM[q] = total.astype(BF16)
            for k in range(1, 4):
                mlp_grad_a_copy(l, k).start()
            UM[l, t] = TM[t]

        def mlp_grad_end(l):
            for k in range(1, 4):
                remote(TM.at[0], UM.at[l, peer_t(k)], gma[l] + k - 1, sib).wait_recv()
            gm_out[l] = UM[l]
            for k in range(1, 4):
                mlp_grad_a_copy(l, k).wait_send()
            mlp_sum[l][3]()

        def mlp_grads(l):
            def product(b, carry):
                lanes = pl.ds(pl.multiple_of(b * 128, 128), 128)
                W2[l, lanes, :] = dot_tn(GY[l, :, lanes], H[l]).astype(BF16)
                W1[l, lanes, :] = dot_tn(N[l, :, lanes], GF[...]).astype(BF16)
                return carry

            lax.fori_loop(0, 6, product, 0)

            def pack(j, carry):
                jc = lax.rem(lax.div(j, 2), 2)
                jq = 2 * lax.div(j, 4) + lax.rem(j, 2)
                at = block(j)
                for b in range(4):
                    lanes = slice(b * 128, b * 128 + 128)
                    GM[l, jc, b, jq, :, 0:128] = W1[l, at, lanes]
                    GM[l, jc, b, jq, :, 256:384] = W2[l, at, lanes]
                for b in range(2):
                    lanes = slice(512 + b * 128, 640 + b * 128)
                    one, two = W1[l, at, lanes].astype(F32), W2[l, at, lanes].astype(F32)
                    GM[l, jc, 2 * b, jq, :, 128:256] = jnp.where(
                        lower, one, pltpu.roll(two, 64, 1)
                    ).astype(BF16)
                    GM[l, jc, 2 * b + 1, jq, :, 128:256] = jnp.where(
                        lower, pltpu.roll(one, 64, 1), two
                    ).astype(BF16)
                return carry

            lax.fori_loop(0, 8, pack, 0)
            mlp_grad_c_copy(l).start()
            SMALL[8 * l + 7 : 8 * l + 8, :] = jnp.sum(GF[...].astype(F32), axis=0, keepdims=True)

        def att_grads(l):
            def product(b, carry):
                lanes = pl.ds(pl.multiple_of(b * 128, 128), 128)
                W1[l, lanes, 0:640] = dot_tn(A[l, :, lanes], G[...]).astype(BF16)
                return carry

            lax.fori_loop(0, 6, product, 0)

            def pack(j, carry):
                jc = lax.rem(lax.div(j, 2), 2)
                jq = 2 * lax.div(j, 4) + lax.rem(j, 2)
                SA[jc, jq] = W1[l, block(j), 0:640]
                return carry

            lax.fori_loop(0, 8, pack, 0)
            att_grad_c_copy(l).start()
            SMALL[8 * l + 6 : 8 * l + 7, 0:640] = jnp.sum(G[...].astype(F32), axis=0, keepdims=True)
            SMALL[8 * l + 6 : 8 * l + 7, 640:768] = jnp.zeros((1, 128), F32)

        def sv_copy(k):
            return remote(SV.at[z], SV.at[z], sv_base + k - 1, {"tensor": z_to(k)})

        def biases_start():
            SV[z] = jnp.zeros((layers, 8, 256), F32)
            for l in range(layers):
                for r in range(6):
                    SV[z, l, r : r + 1, 0:192] = sv[r, l : l + 1, :]
            for k in range(1, 4):
                sv_copy(k).start()

        def biases_ready():
            for k in range(1, 4):
                remote(SV.at[z], SV.at[z_from(k)], sv_base + k - 1, sib).wait_recv()
            for l in range(layers):
                BQ[l, :, 0:256] = SV[t, l, 0:1, :]
                BQ[l, :, 256:384] = jnp.zeros((1, 128), F32)
                BQ[l, :, 384:640] = SV[t, l, 1:2, :]
                hidden = [SV[b, l, pl.ds(2 + t, 1), :] for b in range(4)]
                for b in range(4):
                    B1[l, :, b * 128 : b * 128 + 128] = hidden[b][:, 0:128]
                for b in range(2):
                    even, odd = hidden[2 * b][:, 128:256], hidden[2 * b + 1][:, 128:256]
                    B1[l, :, 512 + b * 128 : 640 + b * 128] = jnp.where(
                        lower, even, pltpu.roll(odd, 64, 1)
                    )
            for k in range(1, 4):
                sv_copy(k).wait_send()

        def sz_copy(k):
            return remote(SMALL, SZ.at[k - 1], sz_base + k - 1, {"tensor": z_to(k)})

        def sc_copy():
            return remote(SZ.at[0], SC, sc_base, sib)

        def sq_copy(k):
            return remote(SP.at[t], SP.at[t], sq_base + k - 1, peer_dev(k))

        def small_z():
            for k in range(1, 4):
                sz_copy(k).start()

        def small_c():
            for k in range(1, 4):
                sz_copy(k).wait_recv()
            SZ[0] = SMALL[...] + SZ[0] + SZ[1] + SZ[2]
            sc_copy().start()

        def small_q():
            sc_copy().wait_recv()
            SP[t] = SZ[0] + SC[...]
            for k in range(1, 4):
                sq_copy(k).start()

        def small_end():
            for k in range(1, 4):
                remote(SC, SP.at[peer_t(k)], sq_base + k - 1, sib).wait_recv()
            z_half = lax.div(z, 2)
            upper = lax.rem(z, 2)
            for l in range(layers):
                at = slice(8 * l, 8 * l + 6)
                total = SP[0, at] + SP[1, at] + SP[2, at] + SP[3, at]
                for r in range(6):
                    shared_out[r, l : l + 1, :] = total[r : r + 1]
                line = slice(8 * l + 6, 8 * l + 7)
                split_out[0, l : l + 1, :] = SP[z, line, 0:192]
                split_out[1, l : l + 1, :] = SP[z, line, 384:576]
                line = slice(8 * l + 7, 8 * l + 8)
                for r in range(4):
                    first = SP[r, line, pl.ds(pl.multiple_of(z * 128, 128), 128)]
                    pair = SP[
                        r, line, pl.ds(pl.multiple_of(512 + z_half * 128, 128), 128)
                    ]
                    pair = jnp.where(upper == 1, pltpu.roll(pair, 64, 1), pair)
                    split_out[2 + r, l : l + 1, 0:128] = first
                    split_out[2 + r, l : l + 1, 128:192] = pair[:, 0:64]
            for k in range(1, 4):
                sz_copy(k).wait_send()
                sq_copy(k).wait_send()
            sc_copy().wait_send()

        def qkv(i, l, gathered):
            def step(k, carry):
                if gathered:
                    ag_wait(i, A, l, k)
                tp = peer_t(k)
                at = rows(tp)
                here = pl.ds(pl.multiple_of(cc * tokens + tp * shard, shard), shard)
                made = dot(A[l, at], WA[l]) + BQ[l]
                q01 = made[:, 0:128].astype(BF16) * jnp.asarray(0.125, BF16)
                qk2 = made[:, 128:256]
                q2 = qk2.astype(BF16) * jnp.asarray(0.125, BF16)
                none = jnp.zeros_like(q01)
                QC[l, tp, 0:128] = jnp.where(lower, q01, none)
                QC[l, tp, 128:256] = jnp.where(lower, none, q01)
                QC[l, tp, 256:384] = jnp.where(lower, q2, none)
                v01 = made[:, 384:512]
                v2 = jnp.where(lower, 0.0, pltpu.roll(made[:, 512:640], 64, 1))
                KV[l, 0, here] = made[:, 256:384].astype(BF16)
                KV[l, 1, here] = pltpu.roll(qk2, 64, 1).astype(BF16)
                KV[l, 2, here] = v01.astype(BF16)
                KV[l, 3, here] = v2.astype(BF16)
                VT[l, cc, 0, :, at] = jnp.transpose(v01).astype(BF16)
                VT[l, cc, 1, :, at] = jnp.transpose(v2).astype(BF16)
                return carry

            lax.fori_loop(0, 4, step, 0)
            kv_copy(l).start()
            vt_copy(l, cc).start()

        def kv_copy(l):
            at = KV.at[l, :, pl.ds(pl.multiple_of(cc * tokens, tokens), tokens)]
            return remote(at, at, kv_base[l], sib)

        def vt_copy(l, c):
            return remote(VT.at[l, c], VT.at[l, c], kv_base[l] + 1, sib)

        def kv_wait(l):
            at = KV.at[l, :, pl.ds(pl.multiple_of((1 - cc) * tokens, tokens), tokens)]
            remote(at, at, kv_base[l], sib).wait_recv()
            vt_copy(l, 1 - cc).wait_recv()

        def kv_drain(l):
            kv_copy(l).wait_send()
            vt_copy(l, cc).wait_send()

        def attend(l, hook=None):
            def weigh(scores):
                highest = jnp.max(scores, axis=0, keepdims=True)
                raised = jnp.exp(scores - highest)
                return raised.astype(BF16), 1.0 / jnp.sum(raised, axis=0, keepdims=True)

            def mix(tile, low):
                return dot(VT[l, 0, tile], low[0:tokens]) + dot(VT[l, 1, tile], low[tokens:])

            def step(s, carry):
                k = back(s)
                tp = peer_t(k)
                low, scale = weigh(dot_nt(KV[l, 0], QC[l, tp, 0:256]))
                E01[l, tp] = low
                RR[l, tp, :, 0:256] = scale
                made = mix(0, low) * scale
                both = jnp.where(top_rows, made[:, 0:128], made[:, 128:256])
                CS[k, 0:shard] = jnp.transpose(both).astype(BF16)
                low, scale = weigh(dot_nt(KV[l, 1], QC[l, tp, 256:384]))
                E2[l, tp] = low
                RR[l, tp, :, 256:384] = scale
                third = jnp.transpose(mix(1, low) * scale)
                half = shard // 2
                third = jnp.where(lower, pltpu.roll(third[0:half], 64, 1), third[half:shard])
                CS[k, shard : shard + half] = third.astype(BF16)

                @pl.when(k > 0)
                def _():
                    context_copy(l, k).start()

                if hook is not None:
                    pl.when(k == 1)(hook)
                return carry

            lax.fori_loop(0, 4, step, 0)
            CX[l, t] = CS[0]

        def context_copy(l, k):
            return remote(CS.at[k], CX.at[l, t], cx_base[l] + k - 1, peer_dev(k))

        def attended(l):
            for k in range(1, 4):
                remote(CS.at[0], CX.at[l, peer_t(k)], cx_base[l] + k - 1, sib).wait_recv()
            for b in range(4):
                CF[l, :, b * 128 : b * 128 + 128] = CX[l, b, 0:shard]
            half = shard // 2
            for b in range(2):
                even = CX[l, 2 * b, shard : shard + half].astype(F32)
                odd = CX[l, 2 * b + 1, shard : shard + half].astype(F32)
                lanes = slice(512 + b * 128, 640 + b * 128)
                first = jnp.where(lower, even, pltpu.roll(odd, 64, 1))
                second = jnp.where(lower, pltpu.roll(even, 64, 1), odd)
                CF[l, 0:half, lanes] = first.astype(BF16)
                CF[l, half:shard, lanes] = second.astype(BF16)
            for k in range(1, 4):
                context_copy(l, k).wait_send()
            return dot_nt(CF[l], WO[l])

        def expand(i_ag, i_rs, l):
            def part(k):
                ag_wait(i_ag, N, l, k)
                at = rows(peer_t(k))
                f = dot(N[l, at], W1[l]) + B1[l]
                cdf = 0.5 * (1.0 + lax.erf(f * (2.0**-0.5)))
                slope = cdf + f * jnp.exp(-0.5 * f * f) * ((2.0 * math.pi) ** -0.5)
                H[l, at] = (f * cdf).astype(BF16)
                DG[l, at] = slope.astype(BF16)
                return dot_nt(H[l, at], W2[l])

            rs_loop(i_rs, forth, part)

        def shrink_back(i_ag, i_rs, l, gathered):
            def part(k):
                if gathered:
                    ag_wait(i_ag, GY, l, k)
                at = rows(peer_t(k))
                g = dot(GY[l, at], W2[l]) * DG[l, at].astype(F32)
                GF[at, :] = g.astype(BF16)
                return dot_nt(GF[at, :], W1[l])

            rs_loop(i_rs, forth, part)

        def context_grad_copy(l, k):
            return remote(CS.at[k], GC.at[l, t], gc_base[l] + k - 1, peer_dev(k))

        def context_grads(l, value):
            GO[l] = value
            made = dot(value, WO[l])
            half = shard // 2
            for b in range(4):
                CX[l, b, 0:shard] = made[:, b * 128 : b * 128 + 128].astype(BF16)
                pair = made[:, 512 + (b // 2) * 128 : 640 + (b // 2) * 128]
                first, second = pair[0:half], pair[half:shard]
                if b % 2 == 0:
                    both = jnp.where(lower, first, pltpu.roll(second, 64, 1))
                else:
                    both = jnp.where(lower, pltpu.roll(first, 64, 1), second)
                CX[l, b, shard : shard + half] = both.astype(BF16)
            for k in (3, 1, 2):
                CS[k] = CX[l, peer_t(k)]
                context_grad_copy(l, k).start()
            GC[l, t] = CX[l, t]

        def attend_back(l, hook):
            GKV[...] = jnp.zeros_like(GKV)
            for tile in range(2):
                for half in range(2):
                    keys = KV[l, tile, half * tokens : (half + 1) * tokens]
                    VT[0, half, tile] = jnp.transpose(keys.astype(F32)).astype(BF16)

            def step(k, carry):
                tp = peer_t(k)
                at = rows(tp)

                @pl.when(k > 0)
                def _():
                    remote(
                        CS.at[0], GC.at[l, tp], gc_base[l] + k - 1, sib
                    ).wait_recv()

                pl.when(k == 1)(hook)
                scale = RR[l, tp]
                r01, r2 = scale[:, 0:256], scale[:, 256:384]
                spread = jnp.where(top_rows, scale[:, 0:128], scale[:, 128:256])
                by_row = jnp.transpose(spread)
                by_row2 = jnp.transpose(jnp.where(top_rows, 0.0, r2))
                c01 = (GC[l, tp, 0:shard].astype(F32) * by_row).astype(BF16)
                third = GC[l, tp, shard : shard + shard // 2].astype(F32)
                third = jnp.concatenate([pltpu.roll(third, 64, 1), third], axis=0)
                c2 = (third * by_row2).astype(BF16)
                none = jnp.zeros_like(c01)
                c01 = jnp.concatenate(
                    [jnp.where(lower, c01, none), jnp.where(lower, none, c01)], axis=0
                )
                made = []
                for tile, low_ref, scale, grad, lanes in (
                    (0, E01, r01, c01, slice(0, 256)),
                    (1, E2, r2, c2, slice(256, 384)),
                ):
                    gp = dot_nt(KV[l, 2 + tile], grad)
                    low = low_ref[l, tp]
                    e = low.astype(F32)
                    inner = scale * jnp.sum(e * gp, axis=0, keepdims=True)
                    gs = (e * (gp - inner)).astype(BF16)
                    GKV[tile] += dot(gs, QC[l, tp, lanes])
                    GKV[2 + tile] += dot(low, grad)
                    made.append(dot(VT[0, 0, tile], gs[0:tokens]) + dot(VT[0, 1, tile], gs[tokens:]))
                both = jnp.where(top_rows, made[0][:, 0:128], made[0][:, 128:256])
                GQ[at, 0:128] = (0.125 * jnp.transpose(both)).astype(BF16)
                third = jnp.where(lower, 0.125 * jnp.transpose(made[1]), 0.0)
                GQ[at, 128:256] = third.astype(BF16)
                return carry

            lax.fori_loop(0, 4, step, 0)
            other = pl.ds(pl.multiple_of((1 - cc) * tokens, tokens), tokens)
            for tile in range(4):
                KVS[tile] = GKV[tile, other].astype(BF16)
            gkv_copy(l).start()
            for k in range(1, 4):
                context_grad_copy(l, k).wait_send()

        def gkv_copy(l):
            return remote(KVS, KVR.at[l], gkv_base[l], sib)

        def heads_back(i, l):
            gkv_copy(l).wait_recv()
            gkv_copy(l).wait_send()

            def part(k):
                at = rows(peer_t(k))
                here = pl.ds(pl.multiple_of(cc * tokens + peer_t(k) * shard, shard), shard)
                k01, k2, v01, v2 = (
                    GKV[tile, here] + KVR[l, tile, at].astype(F32) for tile in range(4)
                )
                G[at, 0:128] = GQ[at, 0:128]
                G[at, 128:256] = (
                    GQ[at, 128:256].astype(F32) + pltpu.roll(k2, 64, 1)
                ).astype(BF16)
                G[at, 256:384] = k01.astype(BF16)
                G[at, 384:512] = v01.astype(BF16)
                G[at, 512:640] = pltpu.roll(v2, 64, 1).astype(BF16)
                return dot_nt(G[at, :], WA[l])

            rs_loop(i, back, part)

        spread_start(frames, X0, 0)
        att_b_start(0)
        att_a_piece(0, 0)
        biases_start()
        mlp_a_start(0)
        for p in range(4):
            spread_pass(X0, 0, p)
        for p in range(4):
            spread_wait(frames, X0, 0, p)
        att_a_first(0)

        def first_norm(k, carry):
            at = rows(k)
            hat, inverse = norm_parts(X0[at, :].astype(F32))
            A[0, at] = (hat * row(0, 0) + row(0, 1)).astype(BF16)
            return carry

        lax.fori_loop(0, 4, first_norm, 0)
        XS[0] = X0[rows(t), :].astype(F32)
        att_a_rest(0)
        out_b_start(0)
        mlp_b_start(0)
        biases_ready()
        att_c_start(0)
        att_ready(0)
        spread_start(cot, GY.at[top], 1)
        for l in range(layers):
            qkv(4 * l + 3, l, l > 0)
            out_a_start(l)
            kv_wait(l)
            if l == 0:
                for p in range(4):
                    spread_pass(GY.at[top], 1, p)
            attend(l, (lambda: mlp_pass(0)) if l == 0 else None)
            out_c_start(l)
            if l > 0:
                mlp_pass(l)
            out_ready(l)
            between = XS[l] + attended(l) + row(l, 2)
            MS[l] = between
            hat, inverse = norm_parts(between)
            ag_start(4 * l, N, l, (hat * row(l, 3) + row(l, 4)).astype(BF16))
            mlp_c_start(l)
            mlp_ready(l)
            if l + 1 < layers:
                att_b_start(l + 1)
                out_b_start(l + 1)
            expand(4 * l, l, l)
            if l + 1 < layers:
                mlp_a_start(l + 1)
                att_a_piece(l + 1, 0)
                att_a_first(l + 1)
                att_a_rest(l + 1)
                mlp_b_start(l + 1)
                total = rs_finish(l)
                stream = MS[l] + total + row(l, 5)
                XS[l + 1] = stream
                hat, inverse = norm_parts(stream)
                normed = (hat * row(l + 1, 0) + row(l + 1, 1)).astype(BF16)
                ag_start(4 * l + 7, A, l + 1, normed)
                att_c_start(l + 1)
                att_ready(l + 1)
            else:
                total = rs_finish(l)
                out_start(0, MS[l] + total + row(l, 5))

        spread_drain(frames, X0, 0)
        for l in range(layers):
            kv_drain(l)
        for p in range(4):
            spread_wait(cot, GY.at[top], 1, p)
        GS[...] = GY[top, rows(t)].astype(F32)
        rs_next = layers
        for l in reversed(range(layers)):
            shrink_back(4 * l + 2, rs_next, l, l < top)
            mlp_grads(l)
            mlp_grad_b(l)
            mlp_sum[l][0]()
            grad = GS[...]
            SMALL[8 * l + 5 : 8 * l + 6, :] = jnp.sum(grad, axis=0, keepdims=True)
            gn = rs_finish(rs_next)
            rs_next += 1
            hat, inverse = norm_parts(MS[l])
            gm = grad + norm_back(gn, hat, inverse, row(l, 3))
            context_grads(l, gm.astype(BF16))
            GS[...] = gm
            SMALL[8 * l + 3 : 8 * l + 4, :] = jnp.sum(gn * hat, axis=0, keepdims=True)
            SMALL[8 * l + 4 : 8 * l + 5, :] = jnp.sum(gn, axis=0, keepdims=True)
            SMALL[8 * l + 2 : 8 * l + 3, :] = jnp.sum(gm, axis=0, keepdims=True)
            if l < top:
                att_grad_a(l + 1)
            out_grads(l)

            def hook(l=l):
                if l == top:
                    out_z[0][1]()
                    out_forward(0, (0, 2))
                out_grad_a(l)

            attend_back(l, hook)
            if l < top:
                att_grad_b(l + 1)
            heads_back(rs_next, l)
            mlp_sum[l][1]()
            att_grads(l)
            out_grad_b(l)
            if l < top:
                att_sum[l + 1][1]()
            if l == 0:
                att_grad_a(l)
            gn = rs_finish(rs_next)
            rs_next += 1
            hat, inverse = norm_parts(XS[l])
            gx = GS[...] + norm_back(gn, hat, inverse, row(l, 0))
            if l > 0:
                ag_start(4 * l - 2, GY, l - 1, gx.astype(BF16))
                GS[...] = gx
            SMALL[8 * l : 8 * l + 1, :] = jnp.sum(gn * hat, axis=0, keepdims=True)
            SMALL[8 * l + 1 : 8 * l + 2, :] = jnp.sum(gn, axis=0, keepdims=True)
            if l == 0:
                small_z()
                out_start(1, gx)
                out_forward(1, (0,))
            else:
                out_grad_end(l)
        small_c()
        if layers > 1:
            mlp_grad_a(1)
        att_grad_b(0)
        out_forward(0, (1, 3))
        if layers > 1:
            mlp_grad_end(1)
        mlp_grad_a(0)
        small_q()
        out_z[1][1]()
        out_forward(1, (2,))
        att_sum[0][1]()
        out_forward(1, (1, 3))
        if layers > 1:
            att_grad_end(1)
        mlp_grad_end(0)
        out_grad_end(0)
        small_end()
        out_finish(0, enc)
        att_grad_end(0)
        out_finish(1, xg)

        spread_drain(cot, GY.at[top], 1)
        for l in range(layers):
            att_drain(l)
            ag_drain(4 * l, N, l)
            out_drain(l)
            if l < top:
                ag_drain(4 * l + 2, GY, l)
            if l > 0:
                ag_drain(4 * l + 3, A, l)

    return kernel


def fused_step(frames, cot, hw, mw, wm, shared, sv):
    layers, rows_of, _ = mw.shape
    tokens, width = frames.shape
    shard = tokens // 4
    numbers = Numbers()
    kernel = make_kernel(layers, tokens, width, numbers)
    two = 2 * tokens
    v = pltpu.VMEM
    scratch = [
        v((layers, shard, width), F32),
        v((layers, shard, width), F32),
        v((layers, tokens, width), BF16),
        v((layers, tokens, width), BF16),
        v((layers, shard, width), BF16),
        v((layers, tokens, width), BF16),
        v((shard, width), F32),
        v((layers, width, 640), BF16),
        v((layers, width, width), BF16),
        v((layers, width, width), BF16),
        v((layers, width, width), BF16),
        v((layers, 4, rows_of, 640), BF16),
        v((layers, 4, rows_of, 256), BF16),
        v((layers, 2, 4, 4, rows_of, width // 2), BF16),
        v((layers, 4, 3 * shard, 128), BF16),
        v((layers, 4, two, 128), BF16),
        v((layers, 2, 2, 128, tokens), BF16),
        v((layers, 4, two, 2 * shard), BF16),
        v((layers, 4, two, shard), BF16),
        v((layers, 4, 1, 3 * shard), F32),
        v((4, 3 * shard // 2, 128), BF16),
        v((layers, 4, 3 * shard // 2, 128), BF16),
        v((layers, shard, width), BF16),
        v((layers, 4, 3 * shard // 2, 128), BF16),
        v((layers, tokens, width), BF16),
        v((layers, tokens, width), BF16),
        v((tokens, width), BF16),
        v((tokens, 256), BF16),
        v((tokens, 640), BF16),
        v((4, two, 128), F32),
        v((4, tokens, 128), BF16),
        v((layers, 4, tokens, 128), BF16),
        v((shard, width), F32),
        v((4, shard, width), BF16),
        v((2, 3, shard, width), BF16),
        v((4, 4, rows_of, width // 2), BF16),
        v((layers, 3, 4, rows_of, width // 2), BF16),
        v((4, rows_of, width // 2), BF16),
        v((layers, 4, rows_of, width // 2), BF16),
        v((layers, 4, rows_of, width // 2), BF16),
        v((layers, rows_of, 640), BF16),
        v((2, 4, rows_of, 640), BF16),
        v((4, rows_of, 640), BF16),
        v((layers, 4, rows_of, 640), BF16),
        v((layers, 3, rows_of, 640), BF16),
        v((2, 4, rows_of, width), BF16),
        v((4, rows_of, width), BF16),
        v((layers, 3, rows_of, width), BF16),
        v((4, rows_of, 256), BF16),
        v((layers, 3, rows_of, 256), BF16),
        v((2, 4, shard, width), BF16),
        v((4, layers, 8, 256), F32),
        v((layers, 1, 640), F32),
        v((layers, 1, width), F32),
        v((8 * layers, width), F32),
        v((3, 8 * layers, width), F32),
        v((8 * layers, width), F32),
        v((4, 8 * layers, width), F32),
        pltpu.SemaphoreType.DMA((numbers.count,)),
        pltpu.SemaphoreType.DMA((numbers.count,)),
        pltpu.SemaphoreType.DMA((4,)),
    ]
    inside = pl.BlockSpec(memory_space=pltpu.VMEM)
    outside = pl.BlockSpec(memory_space=pl.ANY)
    return pl.pallas_call(
        kernel,
        out_shape=(
            jax.ShapeDtypeStruct((4, shard, width), BF16),
            jax.ShapeDtypeStruct((4, shard, width), BF16),
            jax.ShapeDtypeStruct((layers, 3, rows_of, width // 4), BF16),
            jax.ShapeDtypeStruct((layers, rows_of, width // 4), BF16),
            jax.ShapeDtypeStruct((layers, 4, rows_of, width // 2), BF16),
            jax.ShapeDtypeStruct((6, layers, width), F32),
            jax.ShapeDtypeStruct((6, layers, width // 4), F32),
        ),
        in_specs=[outside, outside] + [inside] * 5,
        out_specs=(outside, outside) + (inside,) * 5,
        scratch_shapes=scratch,
        compiler_params=pltpu.CompilerParams(
            collective_id=0, has_side_effects=True, vmem_limit_bytes=63 * 1024 * 1024
        ),
    )(frames, cot, hw, mw, wm, shared, sv)


def adam_update(weight, gradient, first_moment, second, step_rate):
    first_new = beta_one * first_moment + (1.0 - beta_one) * gradient
    second_new = beta_two * second + (1.0 - beta_two) * gradient * gradient
    bias_one = 1.0 - beta_one**STEP
    bias_two = 1.0 - beta_two**STEP
    direction = first_new / bias_one / (jnp.sqrt(second_new / bias_two) + adam_epsilon)
    return (second_new, weight - step_rate * (direction + weight_decay * weight))


RATES = (0.1, 0.1, 0.1, 0.1, 2.0, 0.5)


def finish_kernel(*refs):
    enc, xg, pairs = refs[0:3]
    outs = refs[25:]
    groups, at = [], 3
    for i in range(6):
        packed = i in (2, 3)
        grad = (outs[2 + 3 * i],) if packed else (refs[at],)
        at += 0 if packed else 1
        groups.append(grad + tuple(refs[at : at + 3]))
        at += 3
    for r in range(4):
        total = pairs[0, r].astype(F32)
        third = pltpu.roll(total[:, 128:256], 64, 1)
        outs[8][0, :, r, :] = total[:, 0:192]
        outs[11][0, :, r, 0:128] = total[:, 256:384]
        outs[11][0, :, r, 128:192] = third[:, 0:64]
    outs[0][...] = enc[...].astype(F32)
    outs[1][...] = xg[...].astype(F32)
    for i, (grad, weight, first, second) in enumerate(groups):
        g = grad[...].astype(F32)
        renewed, updated = adam_update(weight[...], g, first[...], second[...], RATES[i])
        if i not in (2, 3):
            outs[2 + 3 * i][...] = g
        outs[3 + 3 * i][...] = renewed
        outs[4 + 3 * i][...] = updated


def finish(enc, xg, pairs, groups):
    layers, _, rows_of, wide = groups[0][0].shape
    tokens, width = enc.shape
    cut = 2 if rows_of % 16 == 0 else 1
    steps = layers * cut
    part = rows_of // cut
    stream = pl.BlockSpec((tokens // steps, width), lambda l, h: (cut * l + h, 0))
    heads = pl.BlockSpec((1, 3, part, wide), lambda l, h: (l, 0, h, 0))
    flat = pl.BlockSpec((1, part, wide), lambda l, h: (l, h, 0))
    grid = pl.BlockSpec((1, part, 4, wide), lambda l, h: (l, h, 0, 0))
    shared = pl.BlockSpec((6, layers, width), lambda l, h: (0, 0, 0))
    split = pl.BlockSpec((6, layers, wide), lambda l, h: (0, 0, 0))
    kinds = (heads, flat, grid, grid, shared, split)
    both = pl.BlockSpec((1, 4, part, 2 * wide), lambda l, h: (l, 0, h, 0))
    shapes = [jax.ShapeDtypeStruct((tokens, width), F32)] * 2
    out_specs = [stream, stream]
    for kind, group in zip(kinds, groups):
        shapes += [jax.ShapeDtypeStruct(group[-1].shape, F32)] * 3
        out_specs += [kind] * 3
    return pl.pallas_call(
        finish_kernel,
        grid=(layers, cut),
        out_shape=shapes,
        in_specs=[stream, stream, both]
        + [kind for kind, group in zip(kinds, groups) for _ in group],
        out_specs=out_specs,
        compiler_params=pltpu.CompilerParams(
            dimension_semantics=("arbitrary", "arbitrary"),
            vmem_limit_bytes=63 * 1024 * 1024,
        ),
    )(enc, xg, pairs, *[v for group in groups for v in group])


def shards(
    frames, cotangent, heads_weight, merge_weight, expand_weight, shrink_weight,
    shared_vectors, split_vectors,
    heads_first, heads_second, merge_first, merge_second, expand_first, expand_second,
    shrink_first, shrink_second, shared_first, shared_second, split_first, split_second,
):
    groups = lax.axis_size("dp") // 4
    width = frames.shape[-1]
    dp_group = [[lo + 4 * h for h in range(groups)] for lo in range(4)]

    def to_kernel(v):
        if groups == 1:
            return v
        part = v.reshape(v.shape[:-1] + (groups, 8, width // (8 * groups)))
        return jnp.swapaxes(part, -3, -2).reshape(v.shape)

    def from_kernel(v):
        if groups == 1:
            return v
        part = v.reshape(v.shape[:-1] + (8, groups, width // (8 * groups)))
        return jnp.swapaxes(part, -3, -2).reshape(v.shape)

    def widen(v, axis):
        if groups == 1:
            return v
        return lax.all_gather(
            v, "dp", axis=axis, tiled=True, axis_index_groups=dp_group
        )

    def narrow(v, axis):
        if groups == 1:
            return v
        return lax.psum_scatter(
            v.astype(BF16),
            "dp",
            scatter_dimension=axis,
            tiled=True,
            axis_index_groups=dp_group,
        ).astype(F32)

    e = jnp.swapaxes(expand_weight.astype(BF16), 1, 2)
    s = jnp.swapaxes(shrink_weight.astype(BF16), 1, 2)
    wm = jnp.concatenate([e, s[..., 128:], s[..., :128]], axis=-1)
    wm = widen(wm, 2)
    hw, mw = jnp.swapaxes(heads_weight, 1, 2), merge_weight
    if groups > 1:
        hw = widen(hw.astype(BF16), 2).astype(F32)
        mw = widen(mw.astype(BF16), 1).astype(F32)

    enc, xg, heads_grad, merge_grad, pairs, shared_grad, split_grad = (
        fused_step(
            to_kernel(frames[0]),
            to_kernel(cotangent[0]),
            hw,
            mw,
            wm,
            jnp.swapaxes(to_kernel(shared_vectors), 0, 1),
            jnp.swapaxes(split_vectors, 0, 1),
        )
    )
    enc, xg = (from_kernel(v.reshape(frames.shape[1:])) for v in (enc, xg))
    heads_grad = narrow(heads_grad, 2)
    merge_grad = narrow(merge_grad, 1)
    pairs = narrow(pairs, 2)
    shared_grad = from_kernel(shared_grad)
    if groups > 1:
        shared_grad = lax.psum(shared_grad, "dp", axis_index_groups=dp_group)
        split_grad = lax.psum(split_grad, "dp", axis_index_groups=dp_group)

    def turned(v):
        return jnp.swapaxes(v, 1, 2)

    def lined(v):
        return jnp.swapaxes(v, 0, 1)

    def same(v):
        return v

    table = (
        (turned, (heads_grad,), heads_weight, heads_first, heads_second),
        (same, (merge_grad,), merge_weight, merge_first, merge_second),
        (same, (), expand_weight, expand_first, expand_second),
        (same, (), shrink_weight, shrink_first, shrink_second),
        (lined, (shared_grad,), shared_vectors, shared_first, shared_second),
        (lined, (split_grad,), split_vectors, split_first, split_second),
    )
    groups_in = [g + tuple(view(v) for v in rest) for view, g, *rest in table]
    done = finish(enc, xg, pairs, groups_in)
    out = [done[0][None], done[1][None]]
    for i, (view, *_) in enumerate(table):
        out += [view(v) for v in done[2 + 3 * i : 5 + 3 * i]]
    return tuple(out)


def solution(mesh):
    rows = ("dp", "seq")
    stream = P("dp", "seq", None)
    wide = P(None, rows, None, "tensor")
    flat = P(None, rows, "tensor")
    split = P(None, None, "tensor")
    return jax.shard_map(
        shards,
        mesh=mesh,
        in_specs=(
            stream, stream, wide, flat, wide, wide, P(), split,
            wide, wide, flat, flat, wide, wide, wide, wide, P(), P(), split, split,
        ),
        out_specs=(stream, stream)
        + (wide,) * 3 + (flat,) * 3 + (wide,) * 6 + (P(),) * 3 + (split,) * 3,
        check_vma=False,
    )
```

time: 1050 us -> 267 us (0.25); the launches traced: 1030 us -> 267 us
  waiting for transfers between devices: 638 us -> 0 us
  Pallas kernels: 0 us -> 264 us
  local copies, waits for them, and re-layouts: 156 us -> 1.55 us
  matrix products: 81.5 us -> 0 us
  blocking collectives: 75.9 us -> 0 us
  other arithmetic: 64.5 us -> 1.02 us
  between operations: 16.5 us -> 0.85 us
    psum x7 -> x0, waiting for transfers between devices: 505 us -> none  [the longest x4 316 us: back_total(): return lax.psum(partial_sum, 'tensor')]
    pallas_call x0 -> x2, Pallas kernels: none -> 264 us  [the longest x1 254 us: fused_step(): pl.pallas_call(kernel, out_shape=(jax.ShapeDtypeStruct((4, shard, width),...]
    unnamed x379 -> x4, local copies, waits for them, and re-layouts: 105 us -> 1.48 us
    dot_general x32 -> x0, matrix products: 76.9 us -> none  [the longest x2 10.5 us: shards(): jnp.einsum('td,df->tf', normed_two, expand_full, preferred_element_type=j...]
    unnamed x22 -> x0, waiting for transfers between devices: 73.9 us -> none
    all_gather x5 -> x0, blocking collectives: 52 us -> none  [the longest x1 18.8 us: shards(): lax.all_gather(merge_weight.astype(jnp.bfloat16), ('dp', 'seq'), axis=1,...]
    all_gather x3 -> x0, waiting for transfers between devices: 31.4 us -> none  [the longest x1 24.5 us: shards(): lax.all_gather(shrink_weight.astype(jnp.bfloat16), ('dp', 'seq'), axis=1,...]
    reduce_scatter x4 -> x0, waiting for transfers between devices: 28.2 us -> none  [the longest x2 19.4 us: shards(): lax.psum_scatter(grad_value.reshape(clip_count, full_frames, local_width)...]
  transfers between devices with their start and end apart: 18 -> 0, of which waited for: 13 -> 0; matrix products, arithmetic and copies ran while one was open for 20% -> 0% of each run, Pallas kernels for 0% -> 0%
where the time goes in v1:
time: 267 us
  Pallas kernels  264 us (99%)
    pallas_call x1, Pallas kernels, fused_step(): pl.pallas_call(kernel, out_shape=(jax.ShapeDtypeStruct((4, shard, width),...  254 us
    pallas_call x1, Pallas kernels, finish(): pl.pallas_call(finish_kernel, grid=(layers, cut), out_shape=shapes, in_sp...  9.72 us

profile of v1, /device:TPU:10, one launch (start us, length us, event | category | flops | bytes accessed | tf_op | source)
XLA Modules:
  0.0 267.1 jit_solution(9416985898410027541)
XLA Ops:
  0.7 0.0 copy-start
  0.7 1.3 copy.48
  2.0 0.0 copy-done
  2.0 0.1 copy.49
  2.2 1.0 pad_maximum_fusion.wm
  3.3 254.0 %shard_map.347 = (bf16[4,128,768]{2,1,0:T(8,128)(2,1)}, bf16[4,128,768]{2,1,0:T(8,128)(2,1)}, bf16[2,3,96,192]{3,2,1,0:T(8,128)(2,1)}, bf16[2,96,192]{2,1,0:T(8,...) custom-call(bf16[512,768]{1,0:T(8,128)(2,1)} %bitcast.37, ...), custom_call_target="tpu_custom_call" | custom-call | tf_op jit(solution)/shard_map/pallas_call | solution.py:1392
  257.2 9.7 %shard_map.348 = (f32[512,768]{1,0:T(8,128)}, f32[512,768]{1,0:T(8,128)}, f32[2,3,96,192]{3,2,1,0:T(8,128)}, f32[2,3,96,192]{3,2,1,0:T(8,128)}, f32[2,3,96,192]{...) custom-call(bf16[512,768]{1,0:T(8,128)(2,1)} %bitcast.35, ...), custom_call_target="tpu_custom_call" | custom-call | tf_op jit(solution)/shard_map/pallas_call | solution.py:1470
  (2 shorter events, 0.1 us)
Async XLA Ops:
  0.7 1.4 copy-start

commit v2 on v1

--- a/solution.py
+++ b/solution.py
@@ -83,7 +83,7 @@
         frames, cot, hw, mw, wm, shared, sv,
         enc, xg, gh_out, go_out, gm_out, shared_out, split_out,
         XS, MS, A, N, GO, GY, GS,
-        WA, WO, W1, W2, GA, GB, GM,
+        WA, WO, W1, W2, T, GA, GB, GM,
         QC, KV, VT, E01, E2, RR, CS, CX, CF, GC, H, DG, GF, GQ, G,
         GKV, KVS, KVR,
         OWN, RSS, RSR,
@@ -1029,6 +1029,15 @@
                 context_copy(l, k).wait_send()
             return dot_nt(CF[l], WO[l])
 
+        def turn(weight, l):
+            def step(b, carry):
+                at = pl.ds(pl.multiple_of(b * 128, 128), 128)
+                wide = jnp.transpose(weight[l, at, :].astype(F32)).astype(BF16)
+                T[0 : wide.shape[0], at] = wide
+                return carry
+
+            lax.fori_loop(0, width // 128, step, 0)
+
         def expand(i_ag, i_rs, l):
             def part(k):
                 ag_wait(i_ag, N, l, k)
@@ -1038,7 +1047,7 @@
                 slope = cdf + f * jnp.exp(-0.5 * f * f) * ((2.0 * math.pi) ** -0.5)
                 H[l, at] = (f * cdf).astype(BF16)
                 DG[l, at] = slope.astype(BF16)
-                return dot_nt(H[l, at], W2[l])
+                return dot(H[l, at], T[...])
 
             rs_loop(i_rs, forth, part)
 
@@ -1049,7 +1058,7 @@
                 at = rows(peer_t(k))
                 g = dot(GY[l, at], W2[l]) * DG[l, at].astype(F32)
                 GF[at, :] = g.astype(BF16)
-                return dot_nt(GF[at, :], W1[l])
+                return dot(GF[at, :], T[...])
 
             rs_loop(i_rs, forth, part)
 
@@ -1152,7 +1161,7 @@
                 G[at, 256:384] = k01.astype(BF16)
                 G[at, 384:512] = v01.astype(BF16)
                 G[at, 512:640] = pltpu.roll(v2, 64, 1).astype(BF16)
-                return dot_nt(G[at, :], WA[l])
+                return dot(G[at, :], T[0:640, :])
 
             rs_loop(i, back, part)
 
@@ -1203,6 +1212,7 @@
             if l + 1 < layers:
                 att_b_start(l + 1)
                 out_b_start(l + 1)
+            turn(W2, l)
             expand(4 * l, l, l)
             if l + 1 < layers:
                 mlp_a_start(l + 1)
@@ -1219,6 +1229,7 @@
                 att_c_start(l + 1)
                 att_ready(l + 1)
             else:
+                turn(W1, l)
                 total = rs_finish(l)
                 out_start(0, MS[l] + total + row(l, 5))
 
@@ -1258,6 +1269,7 @@
             attend_back(l, hook)
             if l < top:
                 att_grad_b(l + 1)
+            turn(WA, l)
             heads_back(rs_next, l)
             mlp_sum[l][1]()
             att_grads(l)
@@ -1280,6 +1292,7 @@
                 out_start(1, gx)
                 out_forward(1, (0,))
             else:
+                turn(W1, l - 1)
                 out_grad_end(l)
         small_c()
         if layers > 1:
@@ -1336,6 +1349,7 @@
         v((layers, width, width), BF16),
         v((layers, width, width), BF16),
         v((layers, width, width), BF16),
+        v((width, width), BF16),
         v((layers, 4, rows_of, 640), BF16),
         v((layers, 4, rows_of, 256), BF16),
         v((layers, 2, 4, 4, rows_of, width // 2), BF16),

time: 267 us -> 266 us (level)
  no operation moved by 1% of the time
where the time goes in v2:
time: 266 us
  Pallas kernels  262 us (98%)
    pallas_call x1, Pallas kernels, fused_step(): pl.pallas_call(kernel, out_shape=(jax.ShapeDtypeStruct((4, shard, width),...  253 us
    pallas_call x1, Pallas kernels, finish(): pl.pallas_call(finish_kernel, grid=(layers, cut), out_shape=shapes, in_sp...  9.72 us

profile of v2, /device:TPU:10, one launch (start us, length us, event | category | flops | bytes accessed | tf_op | source)
XLA Modules:
  0.0 265.9 jit_solution(8569247900015568187)
XLA Ops:
  0.7 0.0 copy-start
  0.7 1.3 copy.48
  2.0 0.0 copy-done
  2.0 0.1 copy.49
  2.2 1.0 pad_maximum_fusion.wm
  3.3 252.7 %shard_map.347 = (bf16[4,128,768]{2,1,0:T(8,128)(2,1)}, bf16[4,128,768]{2,1,0:T(8,128)(2,1)}, bf16[2,3,96,192]{3,2,1,0:T(8,128)(2,1)}, bf16[2,96,192]{2,1,0:T(8,...) custom-call(bf16[512,768]{1,0:T(8,128)(2,1)} %bitcast.37, ...), custom_call_target="tpu_custom_call" | custom-call | tf_op jit(solution)/shard_map/pallas_call | solution.py:1406
  256.0 9.7 %shard_map.348 = (f32[512,768]{1,0:T(8,128)}, f32[512,768]{1,0:T(8,128)}, f32[2,3,96,192]{3,2,1,0:T(8,128)}, f32[2,3,96,192]{3,2,1,0:T(8,128)}, f32[2,3,96,192]{...) custom-call(bf16[512,768]{1,0:T(8,128)(2,1)} %bitcast.35, ...), custom_call_target="tpu_custom_call" | custom-call | tf_op jit(solution)/shard_map/pallas_call | solution.py:1484
  (2 shorter events, 0.1 us)
Async XLA Ops:
  0.7 1.4 copy-start

commit v3 on v2

--- a/solution.py
+++ b/solution.py
@@ -1295,17 +1295,17 @@
                 turn(W1, l - 1)
                 out_grad_end(l)
         small_c()
+        att_grad_b(0)
         if layers > 1:
             mlp_grad_a(1)
-        att_grad_b(0)
         out_forward(0, (1, 3))
-        if layers > 1:
-            mlp_grad_end(1)
-        mlp_grad_a(0)
         small_q()
         out_z[1][1]()
         out_forward(1, (2,))
         att_sum[0][1]()
+        if layers > 1:
+            mlp_grad_end(1)
+        mlp_grad_a(0)
         out_forward(1, (1, 3))
         if layers > 1:
             att_grad_end(1)

time: 266 us -> 266 us (level)
  no operation moved by 1% of the time
where the time goes in v3:
time: 266 us
  Pallas kernels  263 us (99%)
    pallas_call x1, Pallas kernels, fused_step(): pl.pallas_call(kernel, out_shape=(jax.ShapeDtypeStruct((4, shard, width),...  253 us
    pallas_call x1, Pallas kernels, finish(): pl.pallas_call(finish_kernel, grid=(layers, cut), out_shape=shapes, in_sp...  9.72 us

profile of v3, /device:TPU:10, one launch (start us, length us, event | category | flops | bytes accessed | tf_op | source)
XLA Modules:
  0.0 266.0 jit_solution(231266664408174099)
XLA Ops:
  0.7 0.0 copy-start
  0.7 1.3 copy.48
  2.0 0.0 copy-done
  2.0 0.1 copy.49
  2.2 1.0 pad_maximum_fusion.wm
  3.3 252.8 %shard_map.347 = (bf16[4,128,768]{2,1,0:T(8,128)(2,1)}, bf16[4,128,768]{2,1,0:T(8,128)(2,1)}, bf16[2,3,96,192]{3,2,1,0:T(8,128)(2,1)}, bf16[2,96,192]{2,1,0:T(8,...) custom-call(bf16[512,768]{1,0:T(8,128)(2,1)} %bitcast.37, ...), custom_call_target="tpu_custom_call" | custom-call | tf_op jit(solution)/shard_map/pallas_call | solution.py:1406
  256.1 9.7 %shard_map.348 = (f32[512,768]{1,0:T(8,128)}, f32[512,768]{1,0:T(8,128)}, f32[2,3,96,192]{3,2,1,0:T(8,128)}, f32[2,3,96,192]{3,2,1,0:T(8,128)}, f32[2,3,96,192]{...) custom-call(bf16[512,768]{1,0:T(8,128)(2,1)} %bitcast.35, ...), custom_call_target="tpu_custom_call" | custom-call | tf_op jit(solution)/shard_map/pallas_call | solution.py:1484
  (2 shorter events, 0.1 us)
Async XLA Ops:
  0.7 1.4 copy-start
